TPU v7x, 256 devices: a whole 4x4x8 slice. The times are simulated.
256 devices in a mesh: lon: 4 (over x_lo, core), lat: 64 (over y, x_hi, z).
Axes of the slice: x: 4 (x_hi: 2, x_lo: 2; x = x_hi * 2 + x_lo), y: 4, z: 8, core: 2. Of those that a mesh axis runs over, the one named last changes fastest.
Arguments:
- tokens: bfloat16 [2, 384, 192, 512], P(None, 'lat', 'lon'), may hold values from -6 to 6
- cotangent: bfloat16 [2, 384, 192, 512], P(None, 'lat', 'lon'), may hold values from -6 to 6
- norm_gain: float32 [512], replicated, may hold values from 0.5 to 1.5
- qkv_weight: bfloat16 [512, 1536], replicated
- out_weight: bfloat16 [512, 512], replicated, may hold values from -0.25 to 0.25
Outputs:
- layer_out: bfloat16 [2, 384, 192, 512], P(None, 'lat', 'lon')
- grad_tokens: bfloat16 [2, 384, 192, 512], P(None, 'lat', 'lon')
- grad_qkv: float32 [512, 1536], replicated
- grad_out: float32 [512, 512], replicated
- grad_gain: float32 [512], replicated
All inputs are finite; a program needn't handle non-finite values.
Results may differ from a plain program's by a relative error of at most 0.0097.
Values may be sent and summed in bfloat16 or wider, within the bound.
A program may use at most 64 MiB of HBM per device.

v0:
```python
import jax
import jax.numpy as jnp
from jax import lax
from jax.sharding import PartitionSpec as P

HEADS = 8
WIN_LAT = 6
WIN_LON = 12


EPSILON = 1e-05


def shifted_2(value, axis, steps):
    count = lax.axis_size(axis)
    pairs = [(source, (source + steps) % count) for source in range(count)]
    return lax.ppermute(value, axis, pairs)


def norm_parts(tokens):
    widened = tokens.astype(jnp.float32)
    centre = jnp.mean(widened, -1, keepdims=True)
    spread = widened - centre
    inv_std = lax.rsqrt(jnp.mean(spread * spread, -1, keepdims=True) + EPSILON)
    return (widened, spread * inv_std, inv_std)


def to_windows(field_grid):
    levels, lat_rows, lon_cols, feat_width = field_grid.shape
    pieces = field_grid.reshape(
        levels, lat_rows // WIN_LAT, WIN_LAT, lon_cols // WIN_LON, WIN_LON, feat_width
    )
    pieces = pieces.transpose(1, 3, 0, 2, 4, 5)
    return pieces.reshape(-1, levels * WIN_LAT * WIN_LON, feat_width)


def from_windows(stacked, levels, lat_rows, lon_cols):
    feat_width = stacked.shape[-1]
    pieces = stacked.reshape(
        lat_rows // WIN_LAT, lon_cols // WIN_LON, levels, WIN_LAT, WIN_LON, feat_width
    )
    return pieces.transpose(2, 0, 3, 1, 4, 5).reshape(levels, lat_rows, lon_cols, feat_width)


def allowed_pairs(window_flags, win_span):
    offset = jnp.arange(win_span) // WIN_LON % WIN_LAT
    upper_half = offset < WIN_LAT // 2
    same_half = upper_half[:, None] == upper_half[None, :]
    return same_half[None, None] | jnp.logical_not(window_flags)[:, None, None, None]


def split_heads(qkv_rows, head_count):
    win_count, win_span, triple = qkv_rows.shape
    feat_width = triple // 3
    head_dim = feat_width // head_count
    queries = qkv_rows[..., :feat_width].reshape(win_count, win_span, head_count, head_dim)
    keys_part = qkv_rows[..., feat_width : 2 * feat_width].reshape(
        win_count, win_span, head_count, head_dim
    )
    values_part = qkv_rows[..., 2 * feat_width :].reshape(win_count, win_span, head_count, head_dim)
    return (queries, keys_part, values_part)


def attend_forward(tok_windows, qkv_weight, window_flags, head_count):
    win_count, win_span, feat_width = tok_windows.shape
    score_scale = (feat_width // head_count) ** (-0.5)
    qkv_rows = jnp.einsum(
        "bsd,de->bse", tok_windows, qkv_weight, preferred_element_type=jnp.float32
    ).astype(jnp.bfloat16)
    queries, keys_part, values_part = split_heads(qkv_rows, head_count)
    scores = (
        jnp.einsum("bqhe,bkhe->bhqk", queries, keys_part, preferred_element_type=jnp.float32)
        * score_scale
    )
    scores = jnp.where(allowed_pairs(window_flags, win_span), scores, -1e30)
    row_peak = jnp.max(scores, -1, keepdims=True)
    exp_scores = jnp.exp(scores - row_peak)
    attn_probs = (exp_scores / jnp.sum(exp_scores, -1, keepdims=True)).astype(jnp.bfloat16)
    attn_mixed = jnp.einsum(
        "bhqk,bkhe->bqhe", attn_probs, values_part, preferred_element_type=jnp.float32
    )
    attn_mixed = attn_mixed.astype(jnp.bfloat16).reshape(win_count, win_span, feat_width)
    return (qkv_rows, attn_probs, attn_mixed)


def attend_backward(
    tok_windows, cot_windows, qkv_rows, attn_probs, attn_mixed, out_weight, head_count
):
    win_count, win_span, feat_width = tok_windows.shape
    head_dim = feat_width // head_count
    score_scale = head_dim ** (-0.5)
    queries, keys_part, values_part = split_heads(qkv_rows, head_count)
    grad_mixed = jnp.einsum(
        "bse,de->bsd", cot_windows, out_weight, preferred_element_type=jnp.float32
    ).astype(jnp.bfloat16)
    wout_part = jnp.einsum(
        "bsd,bse->de", attn_mixed, cot_windows, preferred_element_type=jnp.float32
    )
    grad_heads = grad_mixed.reshape(win_count, win_span, head_count, head_dim)
    grad_values = jnp.einsum(
        "bhqk,bqhe->bkhe", attn_probs, grad_heads, preferred_element_type=jnp.float32
    )
    grad_probs = jnp.einsum(
        "bqhe,bkhe->bhqk", grad_heads, values_part, preferred_element_type=jnp.float32
    )
    probs_wide = attn_probs.astype(jnp.float32)
    row_total = jnp.sum(grad_probs * probs_wide, -1, keepdims=True)
    grad_scores = (probs_wide * (grad_probs - row_total) * score_scale).astype(jnp.bfloat16)
    grad_queries = jnp.einsum(
        "bhqk,bkhe->bqhe", grad_scores, keys_part, preferred_element_type=jnp.float32
    )
    grad_keys = jnp.einsum(
        "bhqk,bqhe->bkhe", grad_scores, queries, preferred_element_type=jnp.float32
    )
    grad_rows = jnp.concatenate(
        [
            grad_queries.reshape(win_count, win_span, feat_width),
            grad_keys.reshape(win_count, win_span, feat_width),
            grad_values.reshape(win_count, win_span, feat_width),
        ],
        -1,
    ).astype(jnp.bfloat16)
    qkv_part = jnp.einsum("bsd,bse->de", tok_windows, grad_rows, preferred_element_type=jnp.float32)
    return (grad_rows, qkv_part, wout_part)


def on_device(tokens, cotangent, norm_gain, qkv_weight, out_weight):
    levels, lat_rows, lon_cols, feat_width = tokens.shape
    half_lat = WIN_LAT // 2
    half_lon = WIN_LON // 2
    widened, normal_x, inv_std = norm_parts(tokens)
    normed = (normal_x * norm_gain).astype(jnp.bfloat16)

    def roll_in(field_grid, lat_send, lon_send):
        arrived = lat_send(field_grid[..., lat_rows - half_lat :, :, :])
        field_grid = jnp.concatenate([arrived, field_grid[..., : lat_rows - half_lat, :, :]], -3)
        arrived = lon_send(field_grid[..., lon_cols - half_lon :, :])
        return jnp.concatenate([arrived, field_grid[..., : lon_cols - half_lon, :]], -2)

    def roll_out(field_grid, lon_send, lat_send):
        arrived = lon_send(field_grid[..., :half_lon, :])
        field_grid = jnp.concatenate([field_grid[..., half_lon:, :], arrived], -2)
        arrived = lat_send(field_grid[..., :half_lat, :, :])
        return jnp.concatenate([field_grid[..., half_lat:, :, :], arrived], -3)

    shifted = roll_in(
        normed,
        lambda rim_part: shifted_2(rim_part, "lat", 1),
        lambda rim_part: shifted_2(rim_part, "lon", 1),
    )
    tok_windows = to_windows(shifted)
    per_row = lon_cols // WIN_LON
    window_flags = (jnp.arange(tok_windows.shape[0]) < per_row) & (lax.axis_index("lat") == 0)
    qkv_rows, attn_probs, attn_mixed = attend_forward(tok_windows, qkv_weight, window_flags, HEADS)
    proj_rows = jnp.einsum(
        "bsd,de->bse", attn_mixed, out_weight, preferred_element_type=jnp.float32
    ).astype(jnp.bfloat16)
    proj_grid = roll_out(
        from_windows(proj_rows, levels, lat_rows, lon_cols),
        lambda rim_part: shifted_2(rim_part, "lon", -1),
        lambda rim_part: shifted_2(rim_part, "lat", -1),
    )
    layer_out = (widened + proj_grid.astype(jnp.float32)).astype(jnp.bfloat16)
    cot_shift = roll_in(
        cotangent,
        lambda rim_part: shifted_2(rim_part, "lat", 1),
        lambda rim_part: shifted_2(rim_part, "lon", 1),
    )
    cot_windows = to_windows(cot_shift)
    grad_rows, qkv_part, wout_part = attend_backward(
        tok_windows, cot_windows, qkv_rows, attn_probs, attn_mixed, out_weight, HEADS
    )
    grad_windows = jnp.einsum(
        "bse,de->bsd", grad_rows, qkv_weight, preferred_element_type=jnp.float32
    ).astype(jnp.bfloat16)
    grad_normed = roll_out(
        from_windows(grad_windows, levels, lat_rows, lon_cols),
        lambda rim_part: shifted_2(rim_part, "lon", -1),
        lambda rim_part: shifted_2(rim_part, "lat", -1),
    )
    grad_wide = grad_normed.astype(jnp.float32)
    gain_part = jnp.sum(grad_wide * normal_x, axis=(0, 1, 2))
    scaled = grad_wide * norm_gain
    grad_tokens = cotangent.astype(jnp.float32) + inv_std * (
        scaled
        - jnp.mean(scaled, -1, keepdims=True)
        - normal_x * jnp.mean(scaled * normal_x, -1, keepdims=True)
    )
    grad_tokens = grad_tokens.astype(jnp.bfloat16)
    qkv_sum, wout_sum, gain_sum = lax.psum((qkv_part, wout_part, gain_part), ("lon", "lat"))
    token_total = levels * lat_rows * lon_cols * lax.axis_size("lat") * lax.axis_size("lon")
    factor = 1.0 / jnp.sqrt(jnp.float32(token_total))
    return (layer_out, grad_tokens, qkv_sum * factor, wout_sum * factor, gain_sum * factor)


def solution(mesh):
    return jax.shard_map(
        on_device,
        mesh=mesh,
        in_specs=(P(None, "lat", "lon", None), P(None, "lat", "lon", None), P(), P(), P()),
        out_specs=(P(None, "lat", "lon", None), P(None, "lat", "lon", None), P(), P(), P()),
        check_vma=False,
    )
```

profile of v0, /device:TPU:1, one launch (start us, length us, event | category | flops | bytes accessed | tf_op | source)
XLA Modules:
  0.0 377.4 jit_solution(5324335528850767230)
XLA Ops:
  7.2 2.0 fusion.57
  9.2 2.5 collective-permute-start.4
  11.7 1.7 convert_reduce_fusion
  16.6 1.6 collective-permute-start
  19.2 8.3 %collective-permute-done.4 = bf16[2,3,48,512]{3,2,1,0:T(8,128)(2,1)S(1)} collective-permute-done((bf16[2,3,48,512]{3,2,1,0:T(8,128)(2,1)}, bf16[2,3,48,512]{3,2,1,0:T(8,128)(2,1)S(1)}, u32[]{:S(2)}, u32[]{:S(2)}) %collective-permute-start.4) | collective-permute-done | bytes 294944 | tf_op jit(solution)/shard_map/ppermute | solution.py:17
  27.5 2.3 collective-permute-start.5
  29.8 4.1 %collective-permute-done = bf16[2,3,48,512]{3,0,2,1:T(2,128)(2,1)} collective-permute-done((bf16[2,3,48,512]{3,0,2,1:T(2,128)(2,1)}, bf16[2,3,48,512]{3,0,2,1:T(2,128)(2,1)}, u32[]{:S(2)}, u32[]{:S(2)}) %collective-permute-start) | collective-permute-done | bytes 294944 | tf_op jit(solution)/shard_map/ppermute | solution.py:17
  41.6 2.0 fusion.35
  46.3 2.2 copy.70
  48.5 2.2 copy.71
  50.7 2.2 copy.69
  52.9 5.6 %fusion.59 = (f32[4,8,144]{2,1,0:T(8,128)S(1)}, f32[4,8,144,144]{2,3,1,0:T(8,128)}) fusion(pred[4,144,144]{1,2,0:T(8,128)(4,1)} %broadcast_or_fusion, bf16[4,144,8,64]{1,3,2,0:T(8,128)(2,1)} %bitcast.77, bf16[4,144,8,64]{1,3,2,0:T(8,128)(2,1)} %bitcast.79), kind=kOutput, calls=%fused_computation.101 | convolution fusion | flops 87589008 | bytes 3935232 | tf_op jit(solution)/shard_map/sub | solution.py:77
  58.4 2.8 divide_convert_fusion
  62.7 1.9 convolution_convert_fusion.1
  64.6 3.0 fusion.60
  67.5 8.1 %fusion.17 = bf16[4,8,64,144]{3,2,1,0:T(8,128)(2,1)} fusion(bf16[4,144,8,64]{1,3,2,0:T(8,128)(2,1)} %bitcast.78, bf16[4,8,144,144]{2,3,1,0:T(8,128)(2,1)} %copy-done.1, f32[4,8,144,144]{2,3,1,0:T(8,128)} %fusion.60), kind=kOutput, calls=%fused_computation.29 | convolution fusion | flops 89879184 | bytes 5160960 | tf_op jit(solution)/shard_map/bhqk,bqhe->bkhe/dot_general | solution.py:112
  75.7 8.0 %fusion.16 = bf16[4,8,64,144]{3,2,1,0:T(8,128)(2,1)} fusion(bf16[4,144,8,64]{1,3,2,0:T(8,128)(2,1)} %bitcast.80, bf16[4,8,144,144]{2,3,1,0:T(8,128)(2,1)} %copy-done.1, f32[4,8,144,144]{2,3,1,0:T(8,128)} %fusion.60), kind=kOutput, calls=%fused_computation.28 | convolution fusion | flops 89879184 | bytes 5160960 | tf_op jit(solution)/shard_map/bhqk,bkhe->bqhe/dot_general | solution.py:109
  83.6 3.1 convolution_convert_fusion.2
  86.8 2.2 copy.55
  90.2 1.6 copy.53
  91.8 2.5 fusion.18
  94.4 3.1 convolution_bitcast_fusion
  103.4 2.0 collective-permute-start.7
  105.4 1.9 convolution_convert_fusion.4
  109.9 2.8 collective-permute-done.2
  113.5 4.7 %collective-permute-start.3 = (bf16[2,3,48,512]{3,0,2,1:T(2,128)(2,1)S(1)}, bf16[2,3,48,512]{3,0,2,1:T(2,128)(2,1)S(1)}, u32[]{:S(2)}, u32[]{:S(2)}) collective-permute-start(bf16[2,3,48,512]{3,0,2,1:T(2,128)(2,1)S(1)} %get-tuple-element.25), channel_id=1, source_target_pairs={{0,63},{1,0},{2,1},{3,2},{4,3},{5,4},{6,5},{7,6},{8,7},{9,8},{10,9... | collective-permute-start | bytes 884744 | tf_op jit(solution)/shard_map/ppermute | solution.py:17
  118.2 3.3 fusion.31
  121.6 4.2 %collective-permute-done.3 = bf16[2,3,48,512]{3,0,2,1:T(2,128)(2,1)S(1)} collective-permute-done((bf16[2,3,48,512]{3,0,2,1:T(2,128)(2,1)S(1)}, bf16[2,3,48,512]{3,0,2,1:T(2,128)(2,1)S(1)}, u32[]{:S(2)}, u32[]{:S(2)}) %collective-permute-start.3) | collective-permute-done | bytes 294944 | tf_op jit(solution)/shard_map/ppermute | solution.py:17
  125.8 3.2 fusion.33
  130.8 78.3 %psum.23 = f32[512]{0:T(512)S(1)} all-reduce(f32[512]{0:T(512)S(1)} %get-tuple-element.10), channel_id=1, replica_groups=mesh['lon'=4,'lat'=64] {'lon','lat'}, use_global_device_ids=true, to_apply=%region_10.11 | all-reduce | flops 512 | bytes 4096 | tf_op jit(solution)/shard_map/psum | solution.py:190
  209.7 155.8 %all-reduce.3.cloned.1.call-done = (f32[512,1536]{1,0:T(8,128)}, f32[512,512]{1,0:T(8,128)}) async-done(((f32[512,1536]{1,0:T(8,128)}, f32[512,512]{1,0:T(8,128)}), (f32[512,1536]{1,0:T(8,128)}, f32[512,512]{1,0:T(8,128)})) %all-reduce.3.cloned.1.call-update) | async-done | bytes 4194320 | tf_op jit(solution)/shard_map/psum | solution.py:190
  365.5 4.0 %broadcast_multiply_fusion = f32[512,1536]{1,0:T(8,128)} fusion(f32[512,1536]{1,0:T(8,128)} %get-tuple-element.13), kind=kLoop, calls=%fused_computation.27 | loop fusion | flops 786432 | bytes 6291456 | tf_op jit(solution)/shard_map/mul | solution.py:193
  (83 shorter events, 29.9 us)
Async XLA Ops:
  7.2 36.8 %copy-start = (bf16[512,1536]{1,0:T(8,128)(2,1)S(1)}, bf16[512,1536]{1,0:T(8,128)(2,1)}, u32[]{:S(2)}) copy-start(bf16[512,1536]{1,0:T(8,128)(2,1)} %param.8) | copy-start | bytes 4718596
  7.2 6.2 %copy-start.2 = (bf16[2,6,48,512]{3,2,1,0:T(8,128)(2,1)S(1)}, bf16[2,6,48,512]{3,2,1,0:T(8,128)(2,1)}, u32[]{:S(2)}) copy-start(bf16[2,6,48,512]{3,2,1,0:T(8,128)(2,1)} %param.5) | copy-start | bytes 1769476
  7.2 7.3 %copy-start.17 = (f32[512]{0:T(512)S(1)}, f32[512]{0:T(512)}, u32[]{:S(2)}) copy-start(f32[512]{0:T(512)} %param.7) | copy-start | bytes 6148
  7.2 358.3 %all-reduce.3.cloned.1.call-start = ((), (), s32[]{:S(2)}) async-start(), calls=%async_computation | async-start | bytes 8388608 | tf_op jit(solution)/shard_map/psum | solution.py:190
  9.2 18.3 %collective-permute-start.4 = (bf16[2,3,48,512]{3,2,1,0:T(8,128)(2,1)}, bf16[2,3,48,512]{3,2,1,0:T(8,128)(2,1)S(1)}, u32[]{:S(2)}, u32[]{:S(2)}) collective-permute-start(bf16[2,3,48,512]{3,2,1,0:T(8,128)(2,1)} %get-tuple-element.22), channel_id=1, source_target_pairs={{0,1},{1,2},{2,3},{3,4},{4,5},{5,6},{6,7},{7,8},{8,9},{9,10},{10,1... | collective-permute-start | bytes 884744 | tf_op jit(solution)/shard_map/ppermute | solution.py:17
  16.6 21.4 %copy-start.5 = (bf16[2,3,48,512]{3,0,2,1:T(2,128)(2,1)}, bf16[2,3,48,512]{3,0,2,1:T(2,128)(2,1)S(1)}, u32[]{:S(2)}) copy-start(bf16[2,3,48,512]{3,0,2,1:T(2,128)(2,1)S(1)} %get-tuple-element.27) | copy-start | bytes 884740
  16.6 17.2 %collective-permute-start = (bf16[2,3,48,512]{3,0,2,1:T(2,128)(2,1)}, bf16[2,3,48,512]{3,0,2,1:T(2,128)(2,1)}, u32[]{:S(2)}, u32[]{:S(2)}) collective-permute-start(bf16[2,3,48,512]{3,0,2,1:T(2,128)(2,1)} %get-tuple-element.26), channel_id=1, source_target_pairs={{0,1},{1,2},{2,3},{3,4},{4,5},{5,6},{6,7},{7,8},{8,9},{9,10},{10,1... | collective-permute-start | bytes 884744 | tf_op jit(solution)/shard_map/ppermute | solution.py:17
  27.5 11.4 %copy-start.18 = (bf16[512,512]{1,0:T(8,128)(2,1)S(1)}, bf16[512,512]{1,0:T(8,128)(2,1)}, u32[]{:S(2)}) copy-start(bf16[512,512]{1,0:T(8,128)(2,1)} %param.9) | copy-start | bytes 1572868
  27.5 9.4 %collective-permute-start.5 = (bf16[2,6,6,512]{3,2,1,0:T(8,128)(2,1)S(1)}, bf16[2,6,6,512]{3,2,1,0:T(8,128)(2,1)S(1)}, u32[]{:S(2)}, u32[]{:S(2)}) collective-permute-start(bf16[2,6,6,512]{3,2,1,0:T(8,128)(2,1)S(1)} %pad_maximum_fusion.8), channel_id=1, source_target_pairs={{0,64},{64,128},{128,192},{192,0},{1,65},{65,129},{129,193},{193,1... | collective-permute-start | bytes 221192 | tf_op jit(solution)/shard_map/ppermute | solution.py:17
  35.4 6.2 %collective-permute-start.1 = (bf16[2,6,6,512]{3,0,2,1:T(2,128)(2,1)}, bf16[2,6,6,512]{3,0,2,1:T(2,128)(2,1)}, u32[]{:S(2)}, u32[]{:S(2)}) collective-permute-start(bf16[2,6,6,512]{3,0,2,1:T(2,128)(2,1)} %pad_maximum_fusion.9), channel_id=1, source_target_pairs={{0,64},{64,128},{128,192},{192,0},{1,65},{65,129},{129,193},{193,1... | collective-permute-start | bytes 221192 | tf_op jit(solution)/shard_map/ppermute | solution.py:17
  38.0 0.9 copy-start.13
  43.9 1.1 copy-start.15
  61.3 1.4 copy-start.1
  61.3 3.3 copy-start.3
  75.6 8.0 %copy-start.4 = (bf16[4,144,512]{1,2,0:T(8,128)(2,1)S(1)}, bf16[4,144,512]{1,2,0:T(8,128)(2,1)}, u32[]{:S(2)}) copy-start(bf16[4,144,512]{1,2,0:T(8,128)(2,1)} %copy.69) | copy-start | bytes 1769476
  86.8 2.2 copy-start.10
  91.8 2.5 copy-start.11
  91.8 2.5 copy-start.12
  91.8 2.5 copy-start.16
  97.5 1.2 copy-start.8
  97.5 1.4 copy-start.14
  98.6 3.9 %collective-permute-start.6 = (bf16[2,6,6,512]{3,0,2,1:T(2,128)(2,1)S(1)}, bf16[2,6,6,512]{3,0,2,1:T(2,128)(2,1)S(1)}, u32[]{:S(2)}, u32[]{:S(2)}) collective-permute-start(bf16[2,6,6,512]{3,0,2,1:T(2,128)(2,1)S(1)} %slice.89), channel_id=1, source_target_pairs={{0,192},{64,0},{128,64},{192,128},{1,193},{65,1},{129,65},{193,129... | collective-permute-start | bytes 221192 | tf_op jit(solution)/shard_map/ppermute | solution.py:17
  101.6 1.0 copy-start.7
  103.4 14.8 %collective-permute-start.7 = (bf16[2,3,48,512]{3,0,2,1:T(2,128)(2,1)S(1)}, bf16[2,3,48,512]{3,0,2,1:T(2,128)(2,1)S(1)}, u32[]{:S(2)}, u32[]{:S(2)}) collective-permute-start(bf16[2,3,48,512]{3,0,2,1:T(2,128)(2,1)S(1)} %get-tuple-element.21), channel_id=1, source_target_pairs={{0,63},{1,0},{2,1},{3,2},{4,3},{5,4},{6,5},{7,6},{8,7},{9,8},{10,9... | collective-permute-start | bytes 884744 | tf_op jit(solution)/shard_map/ppermute | solution.py:17
  108.4 17.4 %copy-start.6 = (bf16[2,6,48,512]{3,2,1,0:T(8,128)(2,1)S(1)}, bf16[2,6,48,512]{3,2,1,0:T(8,128)(2,1)}, u32[]{:S(2)}) copy-start(bf16[2,6,48,512]{3,2,1,0:T(8,128)(2,1)} %param.6) | copy-start | bytes 1769476
  108.4 4.3 %collective-permute-start.2 = (bf16[2,6,6,512]{3,0,2,1:T(2,128)(2,1)S(1)}, bf16[2,6,6,512]{3,0,2,1:T(2,128)(2,1)S(1)}, u32[]{:S(2)}, u32[]{:S(2)}) collective-permute-start(bf16[2,6,6,512]{3,0,2,1:T(2,128)(2,1)S(1)} %slice.85), channel_id=1, source_target_pairs={{0,192},{64,0},{128,64},{192,128},{1,193},{65,1},{129,65},{193,129... | collective-permute-start | bytes 221192 | tf_op jit(solution)/shard_map/ppermute | solution.py:17
  113.5 12.3 %collective-permute-start.3 = (bf16[2,3,48,512]{3,0,2,1:T(2,128)(2,1)S(1)}, bf16[2,3,48,512]{3,0,2,1:T(2,128)(2,1)S(1)}, u32[]{:S(2)}, u32[]{:S(2)}) collective-permute-start(bf16[2,3,48,512]{3,0,2,1:T(2,128)(2,1)S(1)} %get-tuple-element.25), channel_id=1, source_target_pairs={{0,63},{1,0},{2,1},{3,2},{4,3},{5,4},{6,5},{7,6},{8,7},{9,8},{10,9... | collective-permute-start | bytes 884744 | tf_op jit(solution)/shard_map/ppermute | solution.py:17
  365.5 4.0 %copy-start.9 = (f32[512,512]{1,0:T(8,128)S(1)}, f32[512,512]{1,0:T(8,128)}, u32[]{:S(2)}) copy-start(f32[512,512]{1,0:T(8,128)} %get-tuple-element.14) | copy-start | bytes 3145732
Sparse Core Ops, SparseCore 0:
  101.7 263.7 all-reduce.2
where the time goes:
time: 379 us; the launch traced here: 377 us
  waiting for transfers between devices  176 us (46%)
  blocking collectives  78.3 us (21%)
  matrix products  41.1 us (11%)
  local copies, waits for them, and re-layouts  26.7 us (7%)
  other arithmetic  24.9 us (7%)
  starting transfers between devices  16 us (4%)
  between operations  14.4 us (4%)
    psum x1, waiting for transfers between devices, on_device(): lax.psum((qkv_part, wout_part, gain_part), ('lon', 'lat'))  156 us
    psum x1, blocking collectives, on_device(): lax.psum((qkv_part, wout_part, gain_part), ('lon', 'lat'))  78.3 us
    ppermute x8, waiting for transfers between devices, shifted_2(): return lax.ppermute(value, axis, pairs)  20.2 us
    ppermute x8, starting transfers between devices, shifted_2(): return lax.ppermute(value, axis, pairs)  16 us
    dot_general x1, matrix products, attend_backward(): jnp.einsum('bhqk,bqhe->bkhe', grad_scores, queries, preferred_element_typ...  8.11 us
    dot_general x1, matrix products, attend_backward(): jnp.einsum('bhqk,bkhe->bqhe', grad_scores, keys_part, preferred_element_t...  8 us
  transfers between devices with their start and end apart: 9, of which 6 were waited for; matrix products, arithmetic and copies ran while one was open for 7% of the time, Pallas kernels for 0%

commit v1 on v0

v1 whole, which is shorter than its diff:
```python
import jax
import jax.numpy as jnp
import numpy as np
from jax import lax
from jax.experimental import pallas as pl
from jax.experimental.pallas import tpu as pltpu
from jax.sharding import PartitionSpec as P

MESH = pl.DeviceIdType.MESH
F32 = jnp.float32
BF16 = jnp.bfloat16
EPSILON = 1e-05
D = 512
SPAN = 144
HALF = 72
LEVELS, LATS, LONS = 2, 6, 48
RING = {"x": 4, "y": 4, "z": 8}

RUNS = ((0, 6, 0), (6, 12, 48), (18, 12, 128), (30, 12, 208), (42, 6, 288))
PACKED = 336
UL, LL, LR, UR, S1U, S1L, S2U, S3U, S2L, S3L = 0, 48, 96, 144, 192, 272, 352, 432, 512, 592
STAGED = 672
BASES = (0, 192, 352, 416)


def packing():
    table = np.zeros((PACKED, LEVELS * 3 * LONS), np.float32)
    for first, width, row in RUNS:
        for level in range(LEVELS):
            for lat in range(3):
                for lon in range(width):
                    table[row, (level * 3 + lat) * LONS + first + lon] = 1
                    row += 1
    return table


def gathering():
    table = np.zeros((4, SPAN, 256), np.float32)
    quarter = LEVELS * 3 * 6
    for at, start in enumerate((UL, UR, LL, LR)):
        for row in range(quarter):
            table[0, at * quarter + row, start + row] = 1
    for slot, starts in ((1, (S1U, S1L)), (2, (S2U, S2L)), (3, (S3U, S3L))):
        for at, start in enumerate(starts):
            for row in range(HALF):
                table[slot, at * HALF + row, start - BASES[slot] + row] = 1
    return table


def scattering():
    gather = gathering()
    table = np.zeros((STAGED, 4 * SPAN), np.float32)
    for slot in range(4):
        table[BASES[slot] : BASES[slot] + 256, slot * SPAN : (slot + 1) * SPAN] += gather[slot].T
    return table


def dot(a, b):
    return jnp.dot(a, b, preferred_element_type=F32)


def dot_nt(a, b):
    return lax.dot_general(a, b, (((1,), (1,)), ((), ())), preferred_element_type=F32)


def dot_tn(a, b):
    return lax.dot_general(a, b, (((0,), (0,)), ((), ())), preferred_element_type=F32)


def place():
    lat, lon = lax.axis_index("lat"), lax.axis_index("lon")
    return {"x": lon // 2 + 2 * ((lat // 8) % 2), "y": lat // 16, "z": lat % 8, "core": lon % 2}


def device(at):
    return {"lat": (at["y"] * 2 + at["x"] // 2) * 8 + at["z"], "lon": (at["x"] % 2) * 2 + at["core"]}


def moved(axis, steps):
    at = place()
    if axis == "core":
        at["core"] = 1 - at["core"]
    else:
        at[axis] = (at[axis] + steps + RING[axis]) % RING[axis]
    return device(at)


def grid_moved(lat_steps, lon_steps):
    lat, lon = lax.axis_index("lat"), lax.axis_index("lon")
    return {"lat": (lat + lat_steps + 64) % 64, "lon": (lon + lon_steps + 4) % 4}


def kernel(
    tok_ref, cot_ref, gain_ref, wqkv_ref, wout_ref, pack_ref, unpack_ref, gather_ref, scatter_ref,
    lay_ref, gtok_ref, gqkv_ref, gout_ref, ggain_ref,
    packed, staged, back, arrived, xhat_s, inv_s, tokw, normed, cotw, qkv, gmix, mixed, grows,
    send0, recv0, acc0, send1, recv1, acc1, send2, recv2, send3, recv3, full3, full1, other,
    gain_own, gain_core, gain_x, gain_y, gain_z,
    halo_s, halo_r, back_s, back_r, s0, r0, s1, r1, s2, r2, s3, r3, s4, r4, s5, r5, s6, r6, s7, r7, sg, rg,
):
    pending = []

    def remote(src, dst, send_sem, recv_sem, target):
        return pltpu.make_async_remote_copy(
            src_ref=src, dst_ref=dst, send_sem=send_sem, recv_sem=recv_sem, device_id=target, device_id_type=MESH
        )

    def begin(copy):
        copy.start()
        pending.append(copy)
        return copy

    barrier = pltpu.get_barrier_semaphore()
    friends = [grid_moved(1, 0), grid_moved(-1, 0), grid_moved(0, 1), grid_moved(0, -1), grid_moved(1, 1), grid_moved(-1, -1)]
    friends.append(moved("core", 1))
    for axis in ("x", "y", "z"):
        friends += [moved(axis, step) for step in range(1, RING[axis])]
    for friend in friends:
        pl.semaphore_signal(barrier, inc=1, device_id=friend, device_id_type=MESH)

    me = place()
    lat = lax.axis_index("lat")

    for at, source in enumerate((tok_ref, cot_ref)):
        for half in range(2):
            rows = source[:, 3 * half : 3 * half + 3].reshape(LEVELS * 3 * LONS, D)
            packed[at, half] = dot(pack_ref[...], rows).astype(BF16)
        staged[at, LR : LR + 48] = packed[at, 0, 0:48]
        staged[at, S1L : S1L + 80] = packed[at, 0, 48:128]
        staged[at, S2U : S2U + 160] = packed[at, 1, 128:288]

    pl.semaphore_wait(barrier, len(friends))

    def halo(at):
        routes = (
            (packed.at[at, 1, pl.ds(0, 128)], staged.at[at, pl.ds(UR, 128)], grid_moved(1, 0)),
            (packed.at[at, 0, pl.ds(128, 160)], staged.at[at, pl.ds(S2L, 160)], grid_moved(-1, 0)),
            (packed.at[at, 0, pl.ds(288, 48)], staged.at[at, pl.ds(LL, 48)], grid_moved(0, 1)),
            (packed.at[at, 1, pl.ds(288, 48)], staged.at[at, pl.ds(UL, 48)], grid_moved(1, 1)),
        )
        return [
            begin(remote(src, dst, halo_s.at[at, n], halo_r.at[at, n], target))
            for n, (src, dst, target) in enumerate(routes)
        ]

    tok_halo = halo(0)
    cot_halo = halo(1)
    for copy in tok_halo:
        copy.wait_recv()

    for slot in range(4):
        rows = pl.ds(slot * SPAN, SPAN)
        x = dot(gather_ref[slot], staged[0, BASES[slot] : BASES[slot] + 256])
        tokw[rows] = x.astype(BF16)
        spread = x - jnp.mean(x, -1, keepdims=True)
        inv_std = lax.rsqrt(jnp.mean(spread * spread, -1, keepdims=True) + EPSILON)
        xhat = spread * inv_std
        xhat_s[rows] = xhat
        inv_s[rows] = inv_std
        normed[rows] = (xhat * gain_ref[...]).astype(BF16)

    for part in range(3):
        columns = pl.ds(part * D, D)
        qkv[:, columns] = dot(normed[...], wqkv_ref[:, columns]).astype(BF16)

    for copy in cot_halo:
        copy.wait_recv()
    for slot in range(4):
        rows = pl.ds(slot * SPAN, SPAN)
        cotw[rows] = dot(gather_ref[slot], staged[1, BASES[slot] : BASES[slot] + 256]).astype(BF16)
    gmix[...] = dot_nt(cotw[...], wout_ref[...]).astype(BF16)

    low_lanes = lax.broadcasted_iota(jnp.int32, (SPAN, 128), 1) < 64
    apart = (lax.broadcasted_iota(jnp.int32, (SPAN, SPAN), 0) < HALF) != (
        lax.broadcasted_iota(jnp.int32, (SPAN, SPAN), 1) < HALF
    )

    def stack(block):
        zero = jnp.zeros_like(block)
        return jnp.concatenate([jnp.where(low_lanes, block, zero), jnp.where(low_lanes, zero, block)], 0)

    def unstack(block):
        return jnp.where(low_lanes, block[:SPAN], block[SPAN:])

    def window(slot, _):
        rows = pl.ds(pl.multiple_of(slot * SPAN, SPAN), SPAN)
        cut = ((slot < 2) & (lat == 0)) | ((slot >= 2) & (lat == 63))
        bias = jnp.where(apart & cut, -1e30, 0.0)
        for pair in range(4):
            lanes = pl.ds(pair * 128, 128)
            q = qkv[rows, lanes]
            k = stack(qkv[rows, pl.ds(D + pair * 128, 128)])
            v = stack(qkv[rows, pl.ds(2 * D + pair * 128, 128)])
            gm = gmix[rows, lanes]
            scores = dot_nt(k, q).reshape(2, SPAN, SPAN) + bias
            peak = jnp.max(scores, 1, keepdims=True)
            weights = jnp.exp2((scores - peak) * (0.125 * 1.4426950408889634))
            probs = weights * (1.0 / jnp.sum(weights, 1, keepdims=True))
            probs = probs.astype(BF16)
            flat = probs.reshape(2 * SPAN, SPAN)
            mixed[rows, lanes] = dot_tn(flat, v).astype(BF16)
            gprobs = dot_nt(v, gm).reshape(2, SPAN, SPAN)
            wide = probs.astype(F32)
            total = jnp.sum(wide * gprobs, 1, keepdims=True)
            gscores = (wide * (gprobs - total)).astype(BF16).reshape(2 * SPAN, SPAN)
            grows[rows, lanes] = (dot_tn(gscores, k) * 0.125).astype(BF16)
            grows[rows, pl.ds(D + pair * 128, 128)] = (unstack(dot(gscores, q)) * 0.125).astype(BF16)
            grows[rows, pl.ds(2 * D + pair * 128, 128)] = unstack(dot(flat, gm)).astype(BF16)
        return 0

    lax.fori_loop(0, 4, window, 0)

    orders = (("x", "y"), ("y", "x"), ("x", "y"), ("y", "x"))
    pair_copies = []
    for group in range(4):
        if group < 3:
            total = dot_tn(normed[...], grows[:, group * D : (group + 1) * D])
        else:
            total = dot_tn(mixed[...], cotw[...])
        total = [total[:, n * 128 : (n + 1) * 128].reshape(32, 16, 128) for n in range(4)]
        first = me["core"] == 0
        for n in range(2):
            acc0[group, n * 32 : (n + 1) * 32] = jnp.where(first, total[n], total[n + 2])
            send0[group, n * 32 : (n + 1) * 32] = jnp.where(first, total[n + 2], total[n]).astype(BF16)
        pair_copies.append(begin(remote(send0.at[group], recv0.at[group], s0.at[group], r0.at[group], moved("core", 1))))

    def give_back(at, values):
        back[at] = dot(scatter_ref[...], values).astype(BF16)
        arrived[at, 0, 0:48] = back[at, LR : LR + 48]
        arrived[at, 0, 48:128] = back[at, S1L : S1L + 80]
        arrived[at, 1, 128:288] = back[at, S2U : S2U + 160]
        routes = (
            (back.at[at, pl.ds(UR, 128)], arrived.at[at, 1, pl.ds(0, 128)], grid_moved(-1, 0)),
            (back.at[at, pl.ds(S2L, 160)], arrived.at[at, 0, pl.ds(128, 160)], grid_moved(1, 0)),
            (back.at[at, pl.ds(LL, 48)], arrived.at[at, 0, pl.ds(288, 48)], grid_moved(0, -1)),
            (back.at[at, pl.ds(UL, 48)], arrived.at[at, 1, pl.ds(288, 48)], grid_moved(-1, -1)),
        )
        return [
            begin(remote(src, dst, back_s.at[at, n], back_r.at[at, n], target))
            for n, (src, dst, target) in enumerate(routes)
        ]

    def take_back(at, copies, out):
        for copy in copies:
            copy.wait_recv()
        for half in range(2):
            rows = dot(unpack_ref[...], arrived[at, half]).astype(BF16)
            out[:, 3 * half : 3 * half + 3] = rows.reshape(LEVELS, 3, LONS, D)

    first_copies = []
    for group in range(4):
        axis = orders[group][0]
        pair_copies[group].wait_recv()
        acc0[group] = acc0[group] + recv0[group].astype(F32)
        send1[group] = acc0[group].astype(BF16)
        for step in range(1, 4):
            shard = (me[axis] + step) % 4
            first_copies.append(begin(remote(
                send1.at[group, pl.ds(shard * 16, 16)], recv1.at[group, step - 1],
                s1.at[group, step - 1], r1.at[group, step - 1], moved(axis, step),
            )))

    proj = dot(mixed[...], wout_ref[...]).astype(BF16)
    lay_copies = give_back(0, (tokw[...].astype(F32) + proj.astype(F32)).astype(BF16))

    gnormed = dot_nt(grows[...], wqkv_ref[...]).astype(BF16).astype(F32)
    xhat = xhat_s[...]
    gain_rows = jnp.sum(gnormed * xhat, 0, keepdims=True)
    gain_own[...] = jnp.concatenate(
        [gain_rows[:, n * 128 : (n + 1) * 128] for n in range(4)] + [jnp.zeros((4, 128), F32)], 0
    )
    gain_copies = [begin(remote(gain_own, gain_core, sg.at[0], rg.at[0], moved("core", 1)))]
    scaled = gnormed * gain_ref[...]
    gtok = cotw[...].astype(F32) + inv_s[...] * (
        scaled - jnp.mean(scaled, -1, keepdims=True) - xhat * jnp.mean(scaled * xhat, -1, keepdims=True)
    )
    gtok_copies = give_back(1, gtok.astype(BF16))

    second_copies = []
    for group in range(4):
        first, axis = orders[group]
        for copy in first_copies[group * 3 : group * 3 + 3]:
            copy.wait_recv()
        total = acc0[group, pl.ds(me[first] * 16, 16)]
        for step in range(3):
            total = total + recv1[group, step].astype(F32)
        acc1[group] = total
        send2[group] = total.astype(BF16)
        for step in range(1, 4):
            shard = (me[axis] + step) % 4
            second_copies.append(begin(remote(
                send2.at[group, pl.ds(shard * 4, 4)], recv2.at[group, step - 1],
                s2.at[group, step - 1], r2.at[group, step - 1], moved(axis, step),
            )))

    gain_copies[0].wait_recv()
    gain_x[0] = gain_own[...] + gain_core[...]
    for step in range(1, 4):
        gain_copies.append(begin(remote(gain_x.at[0], gain_x.at[step], sg.at[step], rg.at[step], moved("x", step))))

    third_copies = []
    for group in range(4):
        axis = orders[group][1]
        for copy in second_copies[group * 3 : group * 3 + 3]:
            copy.wait_recv()
        total = acc1[group, pl.ds(me[axis] * 4, 4)]
        for step in range(3):
            total = total + recv2[group, step].astype(F32)
        send3[group] = total.reshape(8, 8, 128)
        for step in range(1, 8):
            shard = (me["z"] + step) % 8
            third_copies.append(begin(remote(
                send3.at[group, shard], recv3.at[group, step - 1],
                s3.at[group, step - 1], r3.at[group, step - 1], moved("z", step),
            )))

    for copy in gain_copies[1:4]:
        copy.wait_recv()
    gain_y[0] = gain_x[0] + gain_x[1] + gain_x[2] + gain_x[3]
    for step in range(1, 4):
        gain_copies.append(begin(remote(gain_y.at[0], gain_y.at[step], sg.at[3 + step], rg.at[3 + step], moved("y", step))))

    factor = 1.0 / np.sqrt(np.float32(147456))
    fourth_copies = []
    for group in range(4):
        for copy in third_copies[group * 7 : group * 7 + 7]:
            copy.wait_recv()
        total = send3[group, me["z"]]
        for step in range(7):
            total = total + recv3[group, step]
        full3[group, me["z"]] = total * factor
        own = full3.at[group, me["z"]]
        for step in range(1, 8):
            fourth_copies.append(begin(remote(own, own, s4.at[group, step - 1], r4.at[group, step - 1], moved("z", step))))

    for copy in gain_copies[4:7]:
        copy.wait_recv()
    gain_z[0] = gain_y[0] + gain_y[1] + gain_y[2] + gain_y[3]
    for step in range(1, 8):
        gain_copies.append(begin(remote(gain_z.at[0], gain_z.at[step], sg.at[6 + step], rg.at[6 + step], moved("z", step))))

    def received(copy_of, axis, step):
        return copy_of((me[axis] + RING[axis] - step) % RING[axis], step)

    def z_copy(group):
        return lambda at, step: remote(
            full3.at[group, at], full3.at[group, at], s4.at[group, step - 1], r4.at[group, step - 1], moved("z", step)
        )

    def second_copy(group):
        first, axis = orders[group]

        def copy_of(at, step):
            block = full1.at[group, pl.ds(me[first] * 16 + at * 4, 4)]
            return remote(block, block, s5.at[group, step - 1], r5.at[group, step - 1], moved(axis, step))

        return copy_of

    def first_copy(group):
        axis = orders[group][0]

        def copy_of(at, step):
            block = full1.at[group, pl.ds(at * 16, 16)]
            return remote(block, block, s6.at[group, step - 1], r6.at[group, step - 1], moved(axis, step))

        return copy_of

    for group in range(4):
        first, axis = orders[group]
        for step in range(1, 8):
            received(z_copy(group), "z", step).wait_recv()
        at = me[first] * 16 + me[axis] * 4
        full1[group, pl.ds(at, 4)] = full3[group].reshape(4, 16, 128).astype(BF16)
        for step in range(1, 4):
            begin(second_copy(group)(me[axis], step))

    for group in range(4):
        first, axis = orders[group]
        for step in range(1, 4):
            received(second_copy(group), axis, step).wait_recv()
        for step in range(1, 4):
            begin(first_copy(group)(me[first], step))

    take_back(0, lay_copies, lay_ref)
    take_back(1, gtok_copies, gtok_ref)

    for copy in gain_copies[7:]:
        copy.wait_recv()
    total = gain_z[0]
    for step in range(1, 8):
        total = total + gain_z[step]
    ggain_ref[...] = total * factor

    last_copies = []
    for group in range(4):
        for step in range(1, 4):
            received(first_copy(group), orders[group][0], step).wait_recv()
        last_copies.append(begin(remote(full1.at[group], other.at[group], s7.at[group], r7.at[group], moved("core", 1))))

    for group in range(4):
        last_copies[group].wait_recv()
        first = me["core"] == 0
        for n in range(2):
            mine = full1[group, n * 32 : (n + 1) * 32].astype(F32).reshape(512, 128)
            theirs = other[group, n * 32 : (n + 1) * 32].astype(F32).reshape(512, 128)
            low, high = jnp.where(first, mine, theirs), jnp.where(first, theirs, mine)
            for at, value in ((n, low), (n + 2, high)):
                if group < 3:
                    gqkv_ref[:, group * D + at * 128 : group * D + (at + 1) * 128] = value
                else:
                    gout_ref[:, at * 128 : (at + 1) * 128] = value

    for copy in pending:
        copy.wait_send()


def on_device(tokens, cotangent, norm_gain, qkv_weight, out_weight):
    pack = packing()
    tables = [jnp.asarray(table, BF16) for table in (pack, pack.T, gathering(), scattering())]
    vmem = pl.BlockSpec(memory_space=pltpu.VMEM)
    dma = pltpu.SemaphoreType.DMA
    rows = 4 * SPAN
    scratch = [
        pltpu.VMEM((2, 2, PACKED, D), BF16),
        pltpu.VMEM((2, STAGED, D), BF16),
        pltpu.VMEM((2, STAGED, D), BF16),
        pltpu.VMEM((2, 2, PACKED, D), BF16),
        pltpu.VMEM((rows, D), F32),
        pltpu.VMEM((rows, 1), F32),
        pltpu.VMEM((rows, D), BF16),
        pltpu.VMEM((rows, D), BF16),
        pltpu.VMEM((rows, D), BF16),
        pltpu.VMEM((rows, 3 * D), BF16),
        pltpu.VMEM((rows, D), BF16),
        pltpu.VMEM((rows, D), BF16),
        pltpu.VMEM((rows, 3 * D), BF16),
        pltpu.VMEM((4, 64, 16, 128), BF16),
        pltpu.VMEM((4, 64, 16, 128), BF16),
        pltpu.VMEM((4, 64, 16, 128), F32),
        pltpu.VMEM((4, 64, 16, 128), BF16),
        pltpu.VMEM((4, 3, 16, 16, 128), BF16),
        pltpu.VMEM((4, 16, 16, 128), F32),
        pltpu.VMEM((4, 16, 16, 128), BF16),
        pltpu.VMEM((4, 3, 4, 16, 128), BF16),
        pltpu.VMEM((4, 8, 8, 128), F32),
        pltpu.VMEM((4, 7, 8, 128), F32),
        pltpu.VMEM((4, 8, 8, 128), F32),
        pltpu.VMEM((4, 64, 16, 128), BF16),
        pltpu.VMEM((4, 64, 16, 128), BF16),
        pltpu.VMEM((8, 128), F32),
        pltpu.VMEM((8, 128), F32),
        pltpu.VMEM((4, 8, 128), F32),
        pltpu.VMEM((4, 8, 128), F32),
        pltpu.VMEM((8, 8, 128), F32),
        dma((2, 4)), dma((2, 4)), dma((2, 4)), dma((2, 4)),
        dma((4,)), dma((4,)),
        dma((4, 3)), dma((4, 3)),
        dma((4, 3)), dma((4, 3)),
        dma((4, 7)), dma((4, 7)),
        dma((4, 7)), dma((4, 7)),
        dma((4, 3)), dma((4, 3)),
        dma((4, 3)), dma((4, 3)),
        dma((4,)), dma((4,)),
        dma((14,)), dma((14,)),
    ]
    layer_out, grad_tokens, grad_qkv, grad_out, grad_gain = pl.pallas_call(
        kernel,
        out_shape=(
            jax.ShapeDtypeStruct(tokens.shape, BF16),
            jax.ShapeDtypeStruct(tokens.shape, BF16),
            jax.ShapeDtypeStruct((D, 3 * D), F32),
            jax.ShapeDtypeStruct((D, D), F32),
            jax.ShapeDtypeStruct((8, 128), F32),
        ),
        in_specs=[vmem] * 9,
        out_specs=(vmem,) * 5,
        scratch_shapes=scratch,
        compiler_params=pltpu.CompilerParams(
            collective_id=0, has_side_effects=True, vmem_limit_bytes=56 * 1024 * 1024
        ),
        name="sublayer",
    )(tokens, cotangent, norm_gain.reshape(1, D), qkv_weight, out_weight, *tables)
    return layer_out, grad_tokens, grad_qkv, grad_out, grad_gain[:4].reshape(D)


def solution(mesh):
    grid = P(None, "lat", "lon", None)
    return jax.shard_map(
        on_device,
        mesh=mesh,
        in_specs=(grid, grid, P(), P(), P()),
        out_specs=(grid, grid, P(), P(), P()),
        check_vma=False,
    )
```

time: 379 us -> 92.8 us (0.24)
  waiting for transfers between devices: 176 us -> 0 us
  Pallas kernels: 0 us -> 82 us
  blocking collectives: 78.3 us -> 0 us
  matrix products: 41.1 us -> 0 us
  other arithmetic: 24.9 us -> 0 us
  local copies, waits for them, and re-layouts: 26.7 us -> 9.91 us
  starting transfers between devices: 16 us -> 0 us
  between operations: 14.4 us -> 0.64 us
    psum x1 -> x0, waiting for transfers between devices: 156 us -> none  [on_device(): lax.psum((qkv_part, wout_part, gain_part), ('lon', 'lat'))]
    pallas_call x0 -> x1, Pallas kernels: none -> 82 us  [on_device(): pl.pallas_call(kernel, out_shape=(jax.ShapeDtypeStruct(tokens.shape, BF16...]
    psum x1 -> x0, blocking collectives: 78.3 us -> none  [on_device(): lax.psum((qkv_part, wout_part, gain_part), ('lon', 'lat'))]
    dot_general x11 -> x0, matrix products: 35.5 us -> none  [the longest x1 8.11 us: attend_backward(): jnp.einsum('bhqk,bqhe->bkhe', grad_scores, queries, preferred_element_typ...]
    ppermute x8 -> x0, waiting for transfers between devices: 20.2 us -> none  [shifted_2(): return lax.ppermute(value, axis, pairs)]
    ppermute x8 -> x0, starting transfers between devices: 16 us -> none  [shifted_2(): return lax.ppermute(value, axis, pairs)]
    reshape x7 -> x1, local copies, waits for them, and re-layouts: 13 us -> 1.26 us  [on_device(): grad_gain[:4].reshape(D)]
    convert_element_type x3 -> x0, other arithmetic: 7.08 us -> none  [the longest x1 3.23 us: on_device(): grad_tokens = grad_tokens.astype(jnp.bfloat16)]
  transfers between devices with their start and end apart: 9 -> 0, of which waited for: 6 -> 0; matrix products, arithmetic and copies ran while one was open for 7% -> 0% of each run, Pallas kernels for 0% -> 0%
where the time goes in v1:
time: 92.8 us; the launch traced here: 92.6 us
  Pallas kernels  82 us (88%)
  local copies, waits for them, and re-layouts  9.91 us (11%)
    pallas_call x1, Pallas kernels, on_device(): pl.pallas_call(kernel, out_shape=(jax.ShapeDtypeStruct(tokens.shape, BF16...  82 us
    unnamed x6, local copies, waits for them, and re-layouts  8.65 us

profile of v1, /device:TPU:1, one launch (start us, length us, event | category | flops | bytes accessed | tf_op | source)
XLA Modules:
  0.0 92.6 jit_solution(1363374218697395749)
XLA Ops:
  0.6 82.0 %sublayer.1 = (bf16[2,6,48,512]{3,2,1,0:T(8,128)(2,1)}, bf16[2,6,48,512]{3,2,1,0:T(8,128)(2,1)}, f32[512,1536]{1,0:T(8,128)}, f32[512,512]{1,0:T(8,128)}, f32[8,128]{1,0:T(8,128)}) custom-call(bf16[2,6,48,512]{3,2,1,0:T(8,128)(2,1)} %tok_ref.1, bf16[2,6,48,512]{3,2,1,0:T(8,128)(2,1)} %cot_ref.1, f32[1,512]{1,0:T(1,128)} %bitcast.3, ...), custom_call_target="tpu_custom_call" | custom-call | tf_op jit(solution)/shard_map/sublayer/pallas_call | solution.py:466
  82.6 1.3 %slice_bitcast_fusion = f32[512]{0:T(512)} fusion(f32[8,128]{1,0:T(8,128)} %get-tuple-element.14), kind=kLoop, calls=%fused_computation | loop fusion | bytes 4096 | tf_op jit(solution)/shard_map/reshape | solution.py:483
  83.9 1.9 %copy.18 = bf16[2,6,48,512]{3,2,1,0:T(8,128)(2,1)} copy(bf16[2,6,48,512]{3,2,1,0:T(8,128)(2,1)} %get-tuple-element.20) | data formatting | bytes 1179648
  85.8 1.9 %copy.19 = bf16[2,6,48,512]{3,2,1,0:T(8,128)(2,1)} copy(bf16[2,6,48,512]{3,2,1,0:T(8,128)(2,1)} %get-tuple-element.21) | data formatting | bytes 1179648
  87.7 0.0 copy-start
  87.7 3.8 %copy.20 = f32[512,1536]{1,0:T(8,128)} copy(f32[512,1536]{1,0:T(8,128)} %get-tuple-element.22) | data formatting | bytes 6291456
  91.6 0.0 copy-done
  91.6 1.0 %copy.21 = f32[512,512]{1,0:T(8,128)} copy(f32[512,512]{1,0:T(8,128)S(1)} %copy-done) | data formatting | bytes 2097152
Async XLA Ops:
  87.7 3.8 %copy-start = (f32[512,512]{1,0:T(8,128)S(1)}, f32[512,512]{1,0:T(8,128)}, u32[]{:S(2)}) copy-start(f32[512,512]{1,0:T(8,128)} %get-tuple-element.23) | copy-start | bytes 3145732

commit v2 on v1

v2 whole, which is shorter than its diff:
```python
import jax
import jax.numpy as jnp
import numpy as np
from jax import lax
from jax.experimental import pallas as pl
from jax.experimental.pallas import tpu as pltpu
from jax.sharding import PartitionSpec as P

MESH = pl.DeviceIdType.MESH
F32 = jnp.float32
BF16 = jnp.bfloat16
EPSILON = 1e-05
D = 512
SPAN = 144
HALF = 72
LEVELS, LATS, LONS = 2, 6, 48
RING = {"x": 4, "y": 4, "z": 8}

RUNS = ((0, 6, 0), (6, 12, 48), (18, 12, 128), (30, 12, 208), (42, 6, 288))
PACKED = 336
UL, LL, LR, UR, S1U, S1L, S2U, S3U, S2L, S3L = 0, 48, 96, 144, 192, 272, 352, 432, 512, 592
STAGED = 672
BASES = (0, 192, 336, 416)
AT_ONCE = (2, 3)


def packing():
    table = np.zeros((PACKED, LEVELS * 3 * LONS), np.float32)
    for first, width, row in RUNS:
        for level in range(LEVELS):
            for lat in range(3):
                for lon in range(width):
                    table[row, (level * 3 + lat) * LONS + first + lon] = 1
                    row += 1
    return table


def gathering():
    table = np.zeros((4, SPAN, 256), np.float32)
    quarter = LEVELS * 3 * 6
    for at, start in enumerate((UL, UR, LL, LR)):
        for row in range(quarter):
            table[0, at * quarter + row, start + row] = 1
    for slot, starts in ((1, (S1U, S1L)), (2, (S2U, S2L)), (3, (S3U, S3L))):
        for at, start in enumerate(starts):
            for row in range(HALF):
                table[slot, at * HALF + row, start - BASES[slot] + row] = 1
    return table


def scattering():
    gather = gathering()
    table = np.zeros((STAGED, 4 * SPAN), np.float32)
    for slot in range(4):
        table[BASES[slot] : BASES[slot] + 256, slot * SPAN : (slot + 1) * SPAN] += gather[slot].T
    return table


def dot(a, b):
    return jnp.dot(a, b, preferred_element_type=F32)


def dot_nt(a, b):
    return lax.dot_general(a, b, (((1,), (1,)), ((), ())), preferred_element_type=F32)


def dot_tn(a, b):
    return lax.dot_general(a, b, (((0,), (0,)), ((), ())), preferred_element_type=F32)


def place():
    lat, lon = lax.axis_index("lat"), lax.axis_index("lon")
    return {"x": (lon >> 1) + 2 * ((lat >> 3) & 1), "y": lat >> 4, "z": lat & 7, "core": lon & 1}


def device(at):
    return {"lat": at["y"] * 16 + (at["x"] >> 1) * 8 + at["z"], "lon": (at["x"] & 1) * 2 + at["core"]}


def targets():
    found = {("core", 1): device(dict(place(), core=1 - place()["core"]))}
    for axis, size in RING.items():
        for step in range(1, size):
            at = place()
            at[axis] = (at[axis] + step) & (size - 1)
            found[axis, step] = device(at)
    lat, lon = lax.axis_index("lat"), lax.axis_index("lon")
    for steps in ((1, 0), (-1, 0), (0, 1), (0, -1), (1, 1), (-1, -1)):
        found[steps] = {"lat": (lat + steps[0]) & 63, "lon": (lon + steps[1]) & 3}
    return found


def kernel(
    tok_hbm, cot_hbm, gain_ref, wqkv_hbm, wout_hbm, pack_hbm, unpack_hbm, gather_hbm, scatter_hbm,
    lay_ref, gtok_ref, grads_ref, ggain_ref,
    tok_ref, cot_ref, wqkv_ref, wout_ref, pack_ref, unpack_ref, gather_ref, scatter_ref, out_s,
    packed, staged, back, arrived, xhat_s, inv_s, tokw, normed, cotw, qkv, gmix, probs_s, mixed, grows,
    send0, recv0, acc0, send1, recv1, acc1, send2, recv2, send3, recv3, full3, all3, full1,
    gain_own, gain_core, gain_x, gain_y, gain_z,
    local_s, halo_s, halo_r, back_s, back_r,
    s0, r0, s1, r1, s2, r2, s3, r3, s4, r4, s5, r5, s6, r6, s7, r7, sg, rg,
):
    pending = []
    locals_out = []

    def remote(src, dst, send_sem, recv_sem, target):
        return pltpu.make_async_remote_copy(
            src_ref=src, dst_ref=dst, send_sem=send_sem, recv_sem=recv_sem, device_id=target, device_id_type=MESH
        )

    def begin(copy):
        copy.start()
        pending.append(copy)
        return copy

    barrier = pltpu.get_barrier_semaphore()
    known = targets()
    friends = list(known.values())

    def moved(axis, step):
        return known[axis, step]

    grid_moved = moved
    loads = {}
    for at, (name, src, dst) in enumerate((
        ("tok", tok_hbm, tok_ref), ("pack", pack_hbm, pack_ref), ("cot", cot_hbm, cot_ref), ("gather", gather_hbm, gather_ref),
        ("wqkv", wqkv_hbm, wqkv_ref), ("wout", wout_hbm, wout_ref), ("scatter", scatter_hbm, scatter_ref), ("unpack", unpack_hbm, unpack_ref),
    )):
        loads[name] = pltpu.make_async_copy(src, dst, local_s.at[at])
        if at < 2:
            loads[name].start()
    for friend in friends:
        pl.semaphore_signal(barrier, inc=1, device_id=friend, device_id_type=MESH)
    for name in ("cot", "gather", "wqkv", "wout", "scatter", "unpack"):
        loads[name].start()

    me = place()
    lat = lax.axis_index("lat")

    def prepare(at, source):
        for half in range(2):
            rows = source[:, 3 * half : 3 * half + 3].reshape(LEVELS * 3 * LONS, D)
            packed[at, half] = dot(pack_ref[...], rows).astype(BF16)
        staged[at, LR : LR + 48] = packed[at, 0, 0:48]
        staged[at, S1L : S1L + 80] = packed[at, 0, 48:128]
        staged[at, S2U : S2U + 160] = packed[at, 1, 128:288]

    def halo(at):
        routes = (
            (packed.at[at, 1, pl.ds(48, 80)], staged.at[at, pl.ds(S1U, 80)], grid_moved(1, 0)),
            (packed.at[at, 0, pl.ds(128, 80)], staged.at[at, pl.ds(S2L, 80)], grid_moved(-1, 0)),
            (packed.at[at, 1, pl.ds(0, 48)], staged.at[at, pl.ds(UR, 48)], grid_moved(1, 0)),
            (packed.at[at, 0, pl.ds(208, 80)], staged.at[at, pl.ds(S3L, 80)], grid_moved(-1, 0)),
            (packed.at[at, 0, pl.ds(288, 48)], staged.at[at, pl.ds(LL, 48)], grid_moved(0, 1)),
            (packed.at[at, 1, pl.ds(288, 48)], staged.at[at, pl.ds(UL, 48)], grid_moved(1, 1)),
        )
        return [
            begin(remote(src, dst, halo_s.at[at, n], halo_r.at[at, n], target))
            for n, (src, dst, target) in enumerate(routes)
        ]

    loads["tok"].wait()
    loads["pack"].wait()
    prepare(0, tok_ref)
    pl.semaphore_wait(barrier, len(friends))
    tok_halo = halo(0)
    loads["cot"].wait()
    prepare(1, cot_ref)
    loads["gather"].wait()
    loads["wqkv"].wait()
    def enter(slot):
        rows = pl.ds(slot * SPAN, SPAN)
        x = dot(gather_ref[slot], staged[0, BASES[slot] : BASES[slot] + 256])
        tokw[rows] = x.astype(BF16)
        spread = x - jnp.mean(x, -1, keepdims=True)
        inv_std = lax.rsqrt(jnp.mean(spread * spread, -1, keepdims=True) + EPSILON)
        xhat = spread * inv_std
        xhat_s[rows] = xhat
        inv_s[rows] = inv_std
        normed[rows] = (xhat * gain_ref[...]).astype(BF16)

    def project(first, second):
        rows = jnp.concatenate([normed[slot * SPAN : (slot + 1) * SPAN] for slot in (first, second)], 0)
        for part in range(3):
            columns = pl.ds(part * D, D)
            both = dot(rows, wqkv_ref[:, columns]).astype(BF16)
            qkv[first * SPAN : (first + 1) * SPAN, columns] = both[:SPAN]
            qkv[second * SPAN : (second + 1) * SPAN, columns] = both[SPAN:]

    low_lanes = lax.broadcasted_iota(jnp.int32, (SPAN, 128), 1) < 64
    apart = (lax.broadcasted_iota(jnp.int32, (SPAN, SPAN), 0) < HALF) != (
        lax.broadcasted_iota(jnp.int32, (SPAN, SPAN), 1) < HALF
    )

    def stack(block):
        zero = jnp.zeros_like(block)
        return jnp.concatenate([jnp.where(low_lanes, block, zero), jnp.where(low_lanes, zero, block)], 0)

    def unstack(block):
        return jnp.where(low_lanes, block[:SPAN], block[SPAN:])

    def rows_of(slot):
        return pl.ds(pl.multiple_of(slot * SPAN, SPAN), SPAN)

    def columns_of(part, pair):
        return pl.ds(part * D + pair * 128, 128)

    def forward(slot, _):
        rows = rows_of(slot)
        cut = ((slot < 2) & (lat == 0)) | ((slot >= 2) & (lat == 63))
        bias = jnp.where(apart & cut, -1e30, 0.0)
        for pair in range(4):
            k = stack(qkv[rows, columns_of(1, pair)])
            scores = dot_nt(k, qkv[rows, columns_of(0, pair)]).reshape(2, SPAN, SPAN) + bias
            peak = jnp.max(scores, 1, keepdims=True)
            weights = jnp.exp2((scores - peak) * (0.125 * 1.4426950408889634))
            probs = weights * (1.0 / jnp.sum(weights, 1, keepdims=True))
            probs = probs.astype(BF16).reshape(2 * SPAN, SPAN)
            probs_s[slot * 4 + pair] = probs
            mixed[rows, columns_of(0, pair)] = dot_tn(probs, stack(qkv[rows, columns_of(2, pair)])).astype(BF16)
        return 0

    for copy in tok_halo[:2]:
        copy.wait_recv()
    cot_halo = halo(1)
    enter(1)
    enter(2)
    project(1, 2)
    lax.fori_loop(0, 2, lambda at, carry: forward(at + 1, carry), 0)
    for copy in tok_halo[2:]:
        copy.wait_recv()
    enter(0)
    enter(3)
    project(0, 3)
    lax.fori_loop(0, 2, lambda at, carry: forward(at * 3, carry), 0)

    loads["wout"].wait()
    for copy in cot_halo:
        copy.wait_recv()
    for slot in range(4):
        rows = pl.ds(slot * SPAN, SPAN)
        cotw[rows] = dot(gather_ref[slot], staged[1, BASES[slot] : BASES[slot] + 256]).astype(BF16)
    gmix[...] = dot_nt(cotw[...], wout_ref[...]).astype(BF16)

    orders = (("x", "y"), ("y", "x"), ("x", "y"), ("y", "x"))
    factor = 1.0 / np.sqrt(np.float32(147456))
    copies = {}
    first_core = me["core"] == 0

    def reduce_pair(group):
        columns = jnp.concatenate([grows[:, part * D + group * 128 : part * D + (group + 1) * 128] for part in range(3)], 1)
        total = dot_tn(normed[...], columns)
        rows = dot_tn(mixed[:, group * 128 : (group + 1) * 128], cotw[...])
        total = [total[:, n * 128 : (n + 1) * 128].reshape(32, 16, 128) for n in range(3)]
        total.append(jnp.concatenate([rows[:, n * 128 : (n + 1) * 128].reshape(8, 16, 128) for n in range(4)], 0))
        for n in range(2):
            acc0[group, n * 32 : (n + 1) * 32] = jnp.where(first_core, total[n], total[n + 2])
            send0[group, n * 32 : (n + 1) * 32] = jnp.where(first_core, total[n + 2], total[n]).astype(BF16)
        copies[0, group] = [begin(remote(send0.at[group], recv0.at[group], s0.at[group], r0.at[group], moved("core", 1)))]

    def settle(phase, group):
        for copy in copies[phase, group]:
            copy.wait_recv()

    def reduce_first(group):
        axis = orders[group][0]
        settle(0, group)
        acc0[group] = acc0[group] + recv0[group].astype(F32)
        send1[group] = acc0[group].astype(BF16)
        copies[1, group] = []
        for step in (2, 1, 3):
            shard = (me[axis] + step) & 3
            copies[1, group].append(begin(remote(
                send1.at[group, pl.ds(shard * 16, 16)], recv1.at[group, step - 1],
                s1.at[group, step - 1], r1.at[group, step - 1], moved(axis, step),
            )))

    def reduce_second(group):
        first, axis = orders[group]
        settle(1, group)
        total = acc0[group, pl.ds(me[first] * 16, 16)]
        for step in range(3):
            total = total + recv1[group, step].astype(F32)
        acc1[group] = total
        send2[group] = total.astype(BF16)
        copies[2, group] = []
        for step in (2, 1, 3):
            shard = (me[axis] + step) & 3
            copies[2, group].append(begin(remote(
                send2.at[group, pl.ds(shard * 4, 4)], recv2.at[group, step - 1],
                s2.at[group, step - 1], r2.at[group, step - 1], moved(axis, step),
            )))

    def reduce_third(group):
        axis = orders[group][1]
        settle(2, group)
        total = acc1[group, pl.ds(me[axis] * 4, 4)]
        for step in range(3):
            total = total + recv2[group, step].astype(F32)
        copies[3, group] = []
        if group in AT_ONCE:
            part = all3.at[group, me["z"]]
            part[...] = (total * factor).astype(BF16)
            for step in (4, 3, 5, 2, 6, 1, 7):
                begin(remote(part, part, s3.at[group, step - 1], r3.at[group, step - 1], moved("z", step)))
            return
        send3[group] = total.reshape(8, 8, 128)
        for step in (4, 3, 5, 2, 6, 1, 7):
            shard = (me["z"] + step) & 7
            copies[3, group].append(begin(remote(
                send3.at[group, shard], recv3.at[group, step - 1],
                s3.at[group, step - 1], r3.at[group, step - 1], moved("z", step),
            )))

    def spread_third(group):
        settle(3, group)
        total = send3[group, me["z"]]
        for step in range(7):
            total = total + recv3[group, step]
        full3[group, me["z"]] = total * factor
        own = full3.at[group, me["z"]]
        for step in (4, 3, 5, 2, 6, 1, 7):
            begin(remote(own, own, s4.at[group, step - 1], r4.at[group, step - 1], moved("z", step)))

    def sender(axis, step):
        return (me[axis] + RING[axis] - step) & (RING[axis] - 1)

    def spread_second(group):
        first, axis = orders[group]
        own = pl.ds(me[first] * 16 + me[axis] * 4, 4)
        buffer, sent, came = (all3, s3, r3) if group in AT_ONCE else (full3, s4, r4)
        for step in (1, 7, 2, 6, 3, 5, 4):
            block = buffer.at[group, sender("z", step)]
            remote(block, block, sent.at[group, step - 1], came.at[group, step - 1], moved("z", step)).wait_recv()
        if group in AT_ONCE:
            total = all3[group, 0].astype(F32)
            for at in range(1, 8):
                total = total + all3[group, at].astype(F32)
            full1[group, own] = total.astype(BF16)
        else:
            full1[group, own] = full3[group].reshape(4, 16, 128).astype(BF16)
        block = full1.at[group, own]
        for step in (2, 1, 3):
            begin(remote(block, block, s5.at[group, step - 1], r5.at[group, step - 1], moved(axis, step)))

    def spread_first(group):
        first, axis = orders[group]
        for step in range(1, 4):
            block = full1.at[group, pl.ds(me[first] * 16 + sender(axis, step) * 4, 4)]
            remote(block, block, s5.at[group, step - 1], r5.at[group, step - 1], moved(axis, step)).wait_recv()
        block = full1.at[group, pl.ds(me[first] * 16, 16)]
        for step in (2, 1, 3):
            begin(remote(block, block, s6.at[group, step - 1], r6.at[group, step - 1], moved(first, step)))
        to_pair(group, me[first], 0)

    def to_pair(group, shard, step):
        rows = pl.ds(shard * 16, 16)
        begin(remote(
            full1.at[group, rows], grads_ref.at[group, me["core"], rows], s7.at[group, step], r7.at[group, step], moved("core", 1)
        ))

    def spread_pair(group):
        axis = orders[group][0]
        for step in (1, 3, 2):
            block = full1.at[group, pl.ds(sender(axis, step) * 16, 16)]
            remote(block, block, s6.at[group, step - 1], r6.at[group, step - 1], moved(axis, step)).wait_recv()
            to_pair(group, sender(axis, step), step)
        keep = pltpu.make_async_copy(full1.at[group], grads_ref.at[group, me["core"]], local_s.at[8 + group])
        keep.start()
        locals_out.append(keep)

    def finish_pair(group):
        axis = orders[group][0]
        for step in range(4):
            rows = pl.ds(sender(axis, step) * 16, 16)
            remote(
                full1.at[group, rows], grads_ref.at[group, 1 - me["core"], rows], s7.at[group, step], r7.at[group, step], moved("core", 1)
            ).wait_recv()

    def give_back(at, values):
        back[at] = dot(scatter_ref[...], values).astype(BF16)
        arrived[at, 0, 0:48] = back[at, LR : LR + 48]
        arrived[at, 0, 48:128] = back[at, S1L : S1L + 80]
        arrived[at, 1, 128:288] = back[at, S2U : S2U + 160]
        routes = (
            (back.at[at, pl.ds(UR, 128)], arrived.at[at, 1, pl.ds(0, 128)], grid_moved(-1, 0)),
            (back.at[at, pl.ds(S2L, 160)], arrived.at[at, 0, pl.ds(128, 160)], grid_moved(1, 0)),
            (back.at[at, pl.ds(LL, 48)], arrived.at[at, 0, pl.ds(288, 48)], grid_moved(0, -1)),
            (back.at[at, pl.ds(UL, 48)], arrived.at[at, 1, pl.ds(288, 48)], grid_moved(-1, -1)),
        )
        return [
            begin(remote(src, dst, back_s.at[at, n], back_r.at[at, n], target))
            for n, (src, dst, target) in enumerate(routes)
        ]

    def take_back(at, arriving, out):
        for copy in arriving:
            copy.wait_recv()
        for half in range(2):
            rows = dot(unpack_ref[...], arrived[at, half]).astype(BF16)
            out_s[at, :, 3 * half : 3 * half + 3] = rows.reshape(LEVELS, 3, LONS, D)
        keep = pltpu.make_async_copy(out_s.at[at], out, local_s.at[12 + at])
        keep.start()
        locals_out.append(keep)

    def gain_copy(src, dst, sem, axis, step):
        return remote(src, dst, sg.at[sem], rg.at[sem], moved(axis, step))

    def gain_send(axis, buffer, value, first):
        own = buffer.at[me[axis]]
        own[...] = value
        for step in range(1, RING[axis]):
            begin(gain_copy(own, own, first + step, axis, step))

    def gain_take(axis, buffer, first):
        for step in range(1, RING[axis]):
            block = buffer.at[sender(axis, step)]
            gain_copy(block, block, first + step, axis, step).wait_recv()
        total = buffer[0]
        for at in range(1, RING[axis]):
            total = total + buffer[at]
        return total

    def backward(pair):
        def two_windows(half, _):
            for slot in (2 * half, 2 * half + 1):
                rows = rows_of(slot)
                probs = probs_s[slot * 4 + pair]
                gm = gmix[rows, columns_of(0, pair)]
                grows[rows, columns_of(2, pair)] = unstack(dot(probs, gm)).astype(BF16)
                gprobs = dot_nt(stack(qkv[rows, columns_of(2, pair)]), gm).reshape(2, SPAN, SPAN)
                wide = probs.astype(F32).reshape(2, SPAN, SPAN)
                total = jnp.sum(wide * gprobs, 1, keepdims=True)
                gscores = (wide * (gprobs - total)).astype(BF16).reshape(2 * SPAN, SPAN)
                grows[rows, columns_of(0, pair)] = (dot_tn(gscores, stack(qkv[rows, columns_of(1, pair)])) * 0.125).astype(BF16)
                grows[rows, columns_of(1, pair)] = (unstack(dot(gscores, qkv[rows, columns_of(0, pair)])) * 0.125).astype(BF16)
            return 0

        lax.fori_loop(0, 2, two_windows, 0)

    proj = dot(mixed[...], wout_ref[...]).astype(BF16)
    loads["scatter"].wait()
    lay_copies = give_back(0, (tokw[...].astype(F32) + proj.astype(F32)).astype(BF16))
    backward(0)
    reduce_pair(0)
    backward(1)
    reduce_pair(1)
    reduce_first(0)
    backward(2)
    reduce_pair(2)
    reduce_first(1)
    backward(3)
    reduce_pair(3)
    reduce_first(2)
    gnormed = dot_nt(grows[...], wqkv_ref[...]).astype(BF16).astype(F32)
    reduce_first(3)
    reduce_second(0)
    xhat = xhat_s[...]
    gain_rows = jnp.sum(gnormed * xhat, 0, keepdims=True)
    gain_own[...] = jnp.concatenate(
        [gain_rows[:, n * 128 : (n + 1) * 128] for n in range(4)] + [jnp.zeros((4, 128), F32)], 0
    )
    begin(gain_copy(gain_own, gain_core, 0, "core", 1))
    scaled = gnormed * gain_ref[...]
    gtok = cotw[...].astype(F32) + inv_s[...] * (
        scaled - jnp.mean(scaled, -1, keepdims=True) - xhat * jnp.mean(scaled * xhat, -1, keepdims=True)
    )
    reduce_second(1)
    gtok_copies = give_back(1, gtok.astype(BF16))
    reduce_second(2)
    reduce_third(0)
    gain_copy(gain_own, gain_core, 0, "core", 1).wait_recv()
    gain_send("x", gain_x, gain_own[...] + gain_core[...], 0)
    reduce_second(3)
    reduce_third(1)
    reduce_third(2)
    gain_send("y", gain_y, gain_take("x", gain_x, 0), 3)
    loads["unpack"].wait()
    take_back(0, lay_copies, lay_ref)
    spread_third(0)
    reduce_third(3)
    spread_third(1)
    gain_send("z", gain_z, gain_take("y", gain_y, 3), 6)
    take_back(1, gtok_copies, gtok_ref)
    for group in (2, 0, 3, 1):
        spread_second(group)
    for group in (2, 0, 3, 1):
        spread_first(group)
    ggain_ref[...] = gain_take("z", gain_z, 6) * factor
    for group in (2, 0, 3, 1):
        spread_pair(group)
    for group in (2, 0, 3, 1):
        finish_pair(group)
    for copy in locals_out:
        copy.wait()
    for copy in pending:
        copy.wait_send()


def unpack_kernel(lay_in, gtok_in, grads_in, gain_in, lay_out, gtok_out, gqkv_out, gout_out, gain_out, narrow, wide, last, grids, sems):
    moves = [pltpu.make_async_copy(grads_in.at[group], narrow.at[group], sems.at[group]) for group in range(4)]
    moves += [pltpu.make_async_copy(source, grids.at[at], sems.at[4 + at]) for at, source in enumerate((lay_in, gtok_in))]
    outs = []
    for at in (4, 5, 0, 1, 2, 3):
        moves[at].start()
    for n in range(4):
        gain_out[:, n * 128 : (n + 1) * 128] = gain_in[n : n + 1]
    for at, target in enumerate((lay_out, gtok_out)):
        moves[4 + at].wait()
        outs.append(pltpu.make_async_copy(grids.at[at], target, sems.at[10 + at]))
        outs[-1].start()
    for group in range(4):
        moves[group].wait()
        for part in range(3):
            tiles = narrow[group, part // 2, (part % 2) * 32 : (part % 2 + 1) * 32]
            columns = pl.ds(part * D + group * 128, 128)
            wide[:, columns] = tiles.astype(F32).reshape(D, 128)
            outs.append(pltpu.make_async_copy(wide.at[:, columns], gqkv_out.at[:, columns], sems.at[12 + group * 3 + part]))
            outs[-1].start()
        for n in range(4):
            tiles = narrow[group, 1, 32 + n * 8 : 32 + (n + 1) * 8]
            last[group * 128 : (group + 1) * 128, n * 128 : (n + 1) * 128] = tiles.astype(F32).reshape(128, 128)
        rows = pl.ds(group * 128, 128)
        outs.append(pltpu.make_async_copy(last.at[rows], gout_out.at[rows], sems.at[6 + group]))
        outs[-1].start()
    for copy in outs:
        copy.wait()


def on_device(tokens, cotangent, norm_gain, qkv_weight, out_weight):
    pack = packing()
    tables = [jnp.asarray(table, BF16) for table in (pack, pack.T, gathering(), scattering())]
    vmem = pl.BlockSpec(memory_space=pltpu.VMEM)
    anywhere = pl.BlockSpec(memory_space=pl.ANY)
    dma = pltpu.SemaphoreType.DMA
    rows = 4 * SPAN
    scratch = [
        pltpu.VMEM(tokens.shape, BF16),
        pltpu.VMEM(tokens.shape, BF16),
        pltpu.VMEM((D, 3 * D), BF16),
        pltpu.VMEM((D, D), BF16),
        *[pltpu.VMEM(table.shape, BF16) for table in tables],
        pltpu.VMEM((2, *tokens.shape), BF16),
        pltpu.VMEM((2, 2, PACKED, D), BF16),
        pltpu.VMEM((2, STAGED, D), BF16),
        pltpu.VMEM((2, STAGED, D), BF16),
        pltpu.VMEM((2, 2, PACKED, D), BF16),
        pltpu.VMEM((rows, D), F32),
        pltpu.VMEM((rows, 1), F32),
        pltpu.VMEM((rows, D), BF16),
        pltpu.VMEM((rows, D), BF16),
        pltpu.VMEM((rows, D), BF16),
        pltpu.VMEM((rows, 3 * D), BF16),
        pltpu.VMEM((rows, D), BF16),
        pltpu.VMEM((16, 2 * SPAN, SPAN), BF16),
        pltpu.VMEM((rows, D), BF16),
        pltpu.VMEM((rows, 3 * D), BF16),
        pltpu.VMEM((4, 64, 16, 128), BF16),
        pltpu.VMEM((4, 64, 16, 128), BF16),
        pltpu.VMEM((4, 64, 16, 128), F32),
        pltpu.VMEM((4, 64, 16, 128), BF16),
        pltpu.VMEM((4, 3, 16, 16, 128), BF16),
        pltpu.VMEM((4, 16, 16, 128), F32),
        pltpu.VMEM((4, 16, 16, 128), BF16),
        pltpu.VMEM((4, 3, 4, 16, 128), BF16),
        pltpu.VMEM((4, 8, 8, 128), F32),
        pltpu.VMEM((4, 7, 8, 128), F32),
        pltpu.VMEM((4, 8, 8, 128), F32),
        pltpu.VMEM((4, 8, 4, 16, 128), BF16),
        pltpu.VMEM((4, 64, 16, 128), BF16),
        pltpu.VMEM((8, 128), F32),
        pltpu.VMEM((8, 128), F32),
        pltpu.VMEM((4, 8, 128), F32),
        pltpu.VMEM((4, 8, 128), F32),
        pltpu.VMEM((8, 8, 128), F32),
        dma((14,)),
        dma((2, 6)), dma((2, 6)), dma((2, 4)), dma((2, 4)),
        dma((4,)), dma((4,)),
        dma((4, 3)), dma((4, 3)),
        dma((4, 3)), dma((4, 3)),
        dma((4, 7)), dma((4, 7)),
        dma((4, 7)), dma((4, 7)),
        dma((4, 3)), dma((4, 3)),
        dma((4, 3)), dma((4, 3)),
        dma((4, 4)), dma((4, 4)),
        dma((14,)), dma((14,)),
    ]
    grid = jax.ShapeDtypeStruct(tokens.shape, BF16)
    parts = pl.pallas_call(
        kernel,
        out_shape=(
            grid,
            grid,
            jax.ShapeDtypeStruct((4, 2, 64, 16, 128), BF16),
            jax.ShapeDtypeStruct((8, 128), F32),
        ),
        in_specs=[anywhere, anywhere, vmem] + [anywhere] * 6,
        out_specs=(anywhere, anywhere, anywhere, vmem),
        scratch_shapes=scratch,
        compiler_params=pltpu.CompilerParams(
            collective_id=0, has_side_effects=True, vmem_limit_bytes=56 * 1024 * 1024
        ),
        name="sublayer",
    )(tokens, cotangent, norm_gain.reshape(1, D), qkv_weight, out_weight, *tables)
    layer_out, grad_tokens, grad_qkv, grad_out, grad_gain = pl.pallas_call(
        unpack_kernel,
        out_shape=(
            grid,
            grid,
            jax.ShapeDtypeStruct((D, 3 * D), F32),
            jax.ShapeDtypeStruct((D, D), F32),
            jax.ShapeDtypeStruct((1, D), F32),
        ),
        in_specs=[anywhere] * 3 + [vmem],
        out_specs=(anywhere,) * 4 + (vmem,),
        scratch_shapes=[pltpu.VMEM((4, 2, 64, 16, 128), BF16), pltpu.VMEM((D, 3 * D), F32), pltpu.VMEM((D, D), F32), pltpu.VMEM((2, *tokens.shape), BF16), dma((24,))],
        compiler_params=pltpu.CompilerParams(vmem_limit_bytes=60 * 1024 * 1024),
        name="results",
    )(*parts)
    return layer_out, grad_tokens, grad_qkv, grad_out, grad_gain.reshape(D)


def solution(mesh):
    grid = P(None, "lat", "lon", None)
    return jax.shard_map(
        on_device,
        mesh=mesh,
        in_specs=(grid, grid, P(), P(), P()),
        out_specs=(grid, grid, P(), P(), P()),
        check_vma=False,
    )
```

time: 92.8 us -> 79.9 us (0.86)
  local copies, waits for them, and re-layouts: 9.91 us -> 0 us
  Pallas kernels: 82 us -> 79 us
    unnamed x6 -> x0, local copies, waits for them, and re-layouts: 8.65 us -> none
    pallas_call x1 -> x2, Pallas kernels: 82 us -> 79 us  [the longest x1 74.1 us: on_device(): pl.pallas_call(kernel, out_shape=(grid, grid, jax.ShapeDtypeStruct((4, 2,...]
    reshape x1 -> x0, local copies, waits for them, and re-layouts: 1.26 us -> none  [on_device(): grad_gain[:4].reshape(D)]
where the time goes in v2:
time: 79.9 us; the launch traced here: 79.8 us
  Pallas kernels  79 us (99%)
  between operations  0.8 us (1%)
    pallas_call x1, Pallas kernels, on_device(): pl.pallas_call(kernel, out_shape=(grid, grid, jax.ShapeDtypeStruct((4, 2,...  74.1 us
    pallas_call x1, Pallas kernels, on_device(): pl.pallas_call(unpack_kernel, out_shape=(grid, grid, jax.ShapeDtypeStruct...  4.89 us

profile of v2, /device:TPU:1, one launch (start us, length us, event | category | flops | bytes accessed | tf_op | source)
XLA Modules:
  0.0 79.8 jit_solution(7592078797308818297)
XLA Ops:
  0.6 74.1 %sublayer.1 = (bf16[2,6,48,512]{3,2,1,0:T(8,128)(2,1)}, bf16[2,6,48,512]{3,2,1,0:T(8,128)(2,1)}, bf16[4,2,64,16,128]{4,3,2,1,0:T(8,128)(2,1)}, f32[8,128]{1,0:T(8,128)}) custom-call(bf16[2,6,48,512]{3,2,1,0:T(8,128)(2,1)} %tok_hbm.1, bf16[2,6,48,512]{3,2,1,0:T(8,128)(2,1)} %cot_hbm.1, f32[1,512]{1,0:T(1,128)} %bitcast.2, bf16[512,1536]{1,0:T(8,128)(2,1)} %wqkv_hbm.1, ...), custom_call_target="tpu_custom_call" | custom-call | tf_op jit(solution)/shard_map/sublayer/pallas_call | solution.py:589
  74.7 4.9 %results.1 = (bf16[2,6,48,512]{3,2,1,0:T(8,128)(2,1)}, bf16[2,6,48,512]{3,2,1,0:T(8,128)(2,1)}, f32[512,1536]{1,0:T(8,128)}, f32[512,512]{1,0:T(8,128)}, f32[1,512]{1,0:T(1,128)}) custom-call(bf16[2,6,48,512]{3,2,1,0:T(8,128)(2,1)} %get-tuple-element.14.lay_in, bf16[2,6,48,512]{3,2,1,0:T(8,128)(2,1)} %get-tuple-element.15.gtok_in, ...), custom_call_target="tpu_custom_call" | custom-call | tf_op jit(solution)/shard_map/results/pallas_call | solution.py:605

commit v3 on v2

--- a/solution.py
+++ b/solution.py
@@ -21,7 +21,6 @@
 UL, LL, LR, UR, S1U, S1L, S2U, S3U, S2L, S3L = 0, 48, 96, 144, 192, 272, 352, 432, 512, 592
 STAGED = 672
 BASES = (0, 192, 336, 416)
-AT_ONCE = (2, 3)
 
 
 def packing():
@@ -95,7 +94,7 @@
     lay_ref, gtok_ref, grads_ref, ggain_ref,
     tok_ref, cot_ref, wqkv_ref, wout_ref, pack_ref, unpack_ref, gather_ref, scatter_ref, out_s,
     packed, staged, back, arrived, xhat_s, inv_s, tokw, normed, cotw, qkv, gmix, probs_s, mixed, grows,
-    send0, recv0, acc0, send1, recv1, acc1, send2, recv2, send3, recv3, full3, all3, full1,
+    send0, recv0, acc0, send1, recv1, acc1, send2, recv2, acc2, send3, recv3, full3, full1,
     gain_own, gain_core, gain_x, gain_y, gain_z,
     local_s, halo_s, halo_r, back_s, back_r,
     s0, r0, s1, r1, s2, r2, s3, r3, s4, r4, s5, r5, s6, r6, s7, r7, sg, rg,
@@ -200,14 +199,14 @@
         return jnp.where(low_lanes, block[:SPAN], block[SPAN:])
 
     def rows_of(slot):
-        return pl.ds(pl.multiple_of(slot * SPAN, SPAN), SPAN)
+        return pl.ds(slot * SPAN, SPAN)
 
     def columns_of(part, pair):
         return pl.ds(part * D + pair * 128, 128)
 
-    def forward(slot, _):
+    def forward(slot):
         rows = rows_of(slot)
-        cut = ((slot < 2) & (lat == 0)) | ((slot >= 2) & (lat == 63))
+        cut = lat == (0 if slot < 2 else 63)
         bias = jnp.where(apart & cut, -1e30, 0.0)
         for pair in range(4):
             k = stack(qkv[rows, columns_of(1, pair)])
@@ -218,7 +217,6 @@
             probs = probs.astype(BF16).reshape(2 * SPAN, SPAN)
             probs_s[slot * 4 + pair] = probs
             mixed[rows, columns_of(0, pair)] = dot_tn(probs, stack(qkv[rows, columns_of(2, pair)])).astype(BF16)
-        return 0
 
     for copy in tok_halo[:2]:
         copy.wait_recv()
@@ -226,13 +224,15 @@
     enter(1)
     enter(2)
     project(1, 2)
-    lax.fori_loop(0, 2, lambda at, carry: forward(at + 1, carry), 0)
+    forward(1)
+    forward(2)
     for copy in tok_halo[2:]:
         copy.wait_recv()
     enter(0)
     enter(3)
     project(0, 3)
-    lax.fori_loop(0, 2, lambda at, carry: forward(at * 3, carry), 0)
+    forward(0)
+    forward(3)
 
     loads["wout"].wait()
     for copy in cot_halo:
@@ -291,57 +291,49 @@
                 s2.at[group, step - 1], r2.at[group, step - 1], moved(axis, step),
             )))
 
-    def reduce_third(group):
-        axis = orders[group][1]
-        settle(2, group)
-        total = acc1[group, pl.ds(me[axis] * 4, 4)]
-        for step in range(3):
-            total = total + recv2[group, step].astype(F32)
-        copies[3, group] = []
-        if group in AT_ONCE:
-            part = all3.at[group, me["z"]]
-            part[...] = (total * factor).astype(BF16)
-            for step in (4, 3, 5, 2, 6, 1, 7):
-                begin(remote(part, part, s3.at[group, step - 1], r3.at[group, step - 1], moved("z", step)))
-            return
-        send3[group] = total.reshape(8, 8, 128)
+    def reduce_third(pair):
+        for at in range(2):
+            group = 2 * pair + at
+            axis = orders[group][1]
+            settle(2, group)
+            total = acc1[group, pl.ds(me[axis] * 4, 4)]
+            for step in range(3):
+                total = total + recv2[group, step].astype(F32)
+            acc2[pair, at * 4 : at * 4 + 4] = total
+            send3[pair, at * 4 : at * 4 + 4] = total.astype(BF16)
+        copies[3, pair] = []
         for step in (4, 3, 5, 2, 6, 1, 7):
             shard = (me["z"] + step) & 7
-            copies[3, group].append(begin(remote(
-                send3.at[group, shard], recv3.at[group, step - 1],
-                s3.at[group, step - 1], r3.at[group, step - 1], moved("z", step),
+            copies[3, pair].append(begin(remote(
+                send3.at[pair, shard], recv3.at[pair, step - 1],
+                s3.at[pair, step - 1], r3.at[pair, step - 1], moved("z", step),
             )))
 
-    def spread_third(group):
-        settle(3, group)
-        total = send3[group, me["z"]]
+    def spread_third(pair):
+        settle(3, pair)
+        total = acc2[pair, me["z"]]
         for step in range(7):
-            total = total + recv3[group, step]
-        full3[group, me["z"]] = total * factor
-        own = full3.at[group, me["z"]]
+            total = total + recv3[pair, step].astype(F32)
+        own = full3.at[pair, me["z"]]
+        own[...] = (total * factor).astype(BF16)
         for step in (4, 3, 5, 2, 6, 1, 7):
-            begin(remote(own, own, s4.at[group, step - 1], r4.at[group, step - 1], moved("z", step)))
+            begin(remote(own, own, s4.at[pair, step - 1], r4.at[pair, step - 1], moved("z", step)))
 
     def sender(axis, step):
         return (me[axis] + RING[axis] - step) & (RING[axis] - 1)
 
-    def spread_second(group):
-        first, axis = orders[group]
-        own = pl.ds(me[first] * 16 + me[axis] * 4, 4)
-        buffer, sent, came = (all3, s3, r3) if group in AT_ONCE else (full3, s4, r4)
+    def spread_second(pair):
         for step in (1, 7, 2, 6, 3, 5, 4):
-            block = buffer.at[group, sender("z", step)]
-            remote(block, block, sent.at[group, step - 1], came.at[group, step - 1], moved("z", step)).wait_recv()
-        if group in AT_ONCE:
-            total = all3[group, 0].astype(F32)
-            for at in range(1, 8):
-                total = total + all3[group, at].astype(F32)
-            full1[group, own] = total.astype(BF16)
-        else:
-            full1[group, own] = full3[group].reshape(4, 16, 128).astype(BF16)
-        block = full1.at[group, own]
-        for step in (2, 1, 3):
-            begin(remote(block, block, s5.at[group, step - 1], r5.at[group, step - 1], moved(axis, step)))
+            block = full3.at[pair, sender("z", step)]
+            remote(block, block, s4.at[pair, step - 1], r4.at[pair, step - 1], moved("z", step)).wait_recv()
+        for at in range(2):
+            group = 2 * pair + at
+            first, axis = orders[group]
+            own = pl.ds(me[first] * 16 + me[axis] * 4, 4)
+            full1[group, own] = full3[pair, at * 4 : at * 4 + 4]
+            block = full1.at[group, own]
+            for step in (2, 1, 3):
+                begin(remote(block, block, s5.at[group, step - 1], r5.at[group, step - 1], moved(axis, step)))
 
     def spread_first(group):
         first, axis = orders[group]
@@ -422,27 +414,23 @@
         return total
 
     def backward(pair):
-        def two_windows(half, _):
-            for slot in (2 * half, 2 * half + 1):
-                rows = rows_of(slot)
-                probs = probs_s[slot * 4 + pair]
-                gm = gmix[rows, columns_of(0, pair)]
-                grows[rows, columns_of(2, pair)] = unstack(dot(probs, gm)).astype(BF16)
-                gprobs = dot_nt(stack(qkv[rows, columns_of(2, pair)]), gm).reshape(2, SPAN, SPAN)
-                wide = probs.astype(F32).reshape(2, SPAN, SPAN)
-                total = jnp.sum(wide * gprobs, 1, keepdims=True)
-                gscores = (wide * (gprobs - total)).astype(BF16).reshape(2 * SPAN, SPAN)
-                grows[rows, columns_of(0, pair)] = (dot_tn(gscores, stack(qkv[rows, columns_of(1, pair)])) * 0.125).astype(BF16)
-                grows[rows, columns_of(1, pair)] = (unstack(dot(gscores, qkv[rows, columns_of(0, pair)])) * 0.125).astype(BF16)
-            return 0
-
-        lax.fori_loop(0, 2, two_windows, 0)
-
+        for slot in range(4):
+            rows = rows_of(slot)
+            probs = probs_s[slot * 4 + pair]
+            gm = gmix[rows, columns_of(0, pair)]
+            grows[rows, columns_of(2, pair)] = unstack(dot(probs, gm)).astype(BF16)
+            gprobs = dot_nt(stack(qkv[rows, columns_of(2, pair)]), gm).reshape(2, SPAN, SPAN)
+            wide = probs.astype(F32).reshape(2, SPAN, SPAN)
+            total = jnp.sum(wide * gprobs, 1, keepdims=True)
+            gscores = (wide * (gprobs - total)).astype(BF16).reshape(2 * SPAN, SPAN)
+            grows[rows, columns_of(0, pair)] = (dot_tn(gscores, stack(qkv[rows, columns_of(1, pair)])) * 0.125).astype(BF16)
+            grows[rows, columns_of(1, pair)] = (unstack(dot(gscores, qkv[rows, columns_of(0, pair)])) * 0.125).astype(BF16)
+
+    backward(0)
+    reduce_pair(0)
     proj = dot(mixed[...], wout_ref[...]).astype(BF16)
     loads["scatter"].wait()
     lay_copies = give_back(0, (tokw[...].astype(F32) + proj.astype(F32)).astype(BF16))
-    backward(0)
-    reduce_pair(0)
     backward(1)
     reduce_pair(1)
     reduce_first(0)
@@ -466,30 +454,32 @@
         scaled - jnp.mean(scaled, -1, keepdims=True) - xhat * jnp.mean(scaled * xhat, -1, keepdims=True)
     )
     reduce_second(1)
-    gtok_copies = give_back(1, gtok.astype(BF16))
+    gain_copy(gain_own, gain_core, 0, "core", 1).wait_recv()
+    gain_send("x", gain_x, gain_own[...] + gain_core[...], 0)
     reduce_second(2)
     reduce_third(0)
-    gain_copy(gain_own, gain_core, 0, "core", 1).wait_recv()
-    gain_send("x", gain_x, gain_own[...] + gain_core[...], 0)
     reduce_second(3)
-    reduce_third(1)
-    reduce_third(2)
     gain_send("y", gain_y, gain_take("x", gain_x, 0), 3)
     loads["unpack"].wait()
     take_back(0, lay_copies, lay_ref)
+    reduce_third(1)
+    gtok_copies = give_back(1, gtok.astype(BF16))
     spread_third(0)
-    reduce_third(3)
+    gain_send("z", gain_z, gain_take("y", gain_y, 3), 6)
     spread_third(1)
-    gain_send("z", gain_z, gain_take("y", gain_y, 3), 6)
+    spread_second(0)
+    spread_second(1)
+    spread_first(0)
+    spread_first(1)
+    spread_first(2)
+    spread_first(3)
     take_back(1, gtok_copies, gtok_ref)
-    for group in (2, 0, 3, 1):
-        spread_second(group)
-    for group in (2, 0, 3, 1):
-        spread_first(group)
     ggain_ref[...] = gain_take("z", gain_z, 6) * factor
-    for group in (2, 0, 3, 1):
-        spread_pair(group)
-    for group in (2, 0, 3, 1):
+    spread_pair(0)
+    spread_pair(1)
+    spread_pair(2)
+    spread_pair(3)
+    for group in range(4):
         finish_pair(group)
     for copy in locals_out:
         copy.wait()
@@ -563,10 +553,10 @@
         pltpu.VMEM((4, 16, 16, 128), F32),
         pltpu.VMEM((4, 16, 16, 128), BF16),
         pltpu.VMEM((4, 3, 4, 16, 128), BF16),
-        pltpu.VMEM((4, 8, 8, 128), F32),
-        pltpu.VMEM((4, 7, 8, 128), F32),
-        pltpu.VMEM((4, 8, 8, 128), F32),
-        pltpu.VMEM((4, 8, 4, 16, 128), BF16),
+        pltpu.VMEM((2, 8, 16, 128), F32),
+        pltpu.VMEM((2, 8, 16, 128), BF16),
+        pltpu.VMEM((2, 7, 16, 128), BF16),
+        pltpu.VMEM((2, 8, 16, 128), BF16),
         pltpu.VMEM((4, 64, 16, 128), BF16),
         pltpu.VMEM((8, 128), F32),
         pltpu.VMEM((8, 128), F32),
@@ -578,8 +568,8 @@
         dma((4,)), dma((4,)),
         dma((4, 3)), dma((4, 3)),
         dma((4, 3)), dma((4, 3)),
-        dma((4, 7)), dma((4, 7)),
-        dma((4, 7)), dma((4, 7)),
+        dma((2, 7)), dma((2, 7)),
+        dma((2, 7)), dma((2, 7)),
         dma((4, 3)), dma((4, 3)),
         dma((4, 3)), dma((4, 3)),
         dma((4, 4)), dma((4, 4)),

time: 79.9 us -> 76.5 us (0.957)
  Pallas kernels: 79 us -> 75.5 us
    pallas_call x1, Pallas kernels: 74.1 us -> 70.6 us  [on_device(): pl.pallas_call(kernel, out_shape=(grid, grid, jax.ShapeDtypeStruct((4, 2,...]
where the time goes in v3:
time: 76.5 us; the launch traced here: 76.3 us
  Pallas kernels  75.5 us (99%)
  between operations  0.8 us (1%)
    pallas_call x1, Pallas kernels, on_device(): pl.pallas_call(kernel, out_shape=(grid, grid, jax.ShapeDtypeStruct((4, 2,...  70.6 us
    pallas_call x1, Pallas kernels, on_device(): pl.pallas_call(unpack_kernel, out_shape=(grid, grid, jax.ShapeDtypeStruct...  4.89 us

profile of v3, /device:TPU:1, one launch (start us, length us, event | category | flops | bytes accessed | tf_op | source)
XLA Modules:
  0.0 76.3 jit_solution(11826068810979375801)
XLA Ops:
  0.6 70.6 %sublayer.1 = (bf16[2,6,48,512]{3,2,1,0:T(8,128)(2,1)}, bf16[2,6,48,512]{3,2,1,0:T(8,128)(2,1)}, bf16[4,2,64,16,128]{4,3,2,1,0:T(8,128)(2,1)}, f32[8,128]{1,0:T(8,128)}) custom-call(bf16[2,6,48,512]{3,2,1,0:T(8,128)(2,1)} %tok_hbm.1, bf16[2,6,48,512]{3,2,1,0:T(8,128)(2,1)} %cot_hbm.1, f32[1,512]{1,0:T(1,128)} %bitcast.2, bf16[512,1536]{1,0:T(8,128)(2,1)} %wqkv_hbm.1, ...), custom_call_target="tpu_custom_call" | custom-call | tf_op jit(solution)/shard_map/sublayer/pallas_call | solution.py:579
  71.3 4.9 %results.1 = (bf16[2,6,48,512]{3,2,1,0:T(8,128)(2,1)}, bf16[2,6,48,512]{3,2,1,0:T(8,128)(2,1)}, f32[512,1536]{1,0:T(8,128)}, f32[512,512]{1,0:T(8,128)}, f32[1,512]{1,0:T(1,128)}) custom-call(bf16[2,6,48,512]{3,2,1,0:T(8,128)(2,1)} %get-tuple-element.14.lay_in, bf16[2,6,48,512]{3,2,1,0:T(8,128)(2,1)} %get-tuple-element.15.gtok_in, ...), custom_call_target="tpu_custom_call" | custom-call | tf_op jit(solution)/shard_map/results/pallas_call | solution.py:595

commit v4 on v3

--- a/solution.py
+++ b/solution.py
@@ -218,9 +218,9 @@
             probs_s[slot * 4 + pair] = probs
             mixed[rows, columns_of(0, pair)] = dot_tn(probs, stack(qkv[rows, columns_of(2, pair)])).astype(BF16)
 
+    cot_halo = halo(1)
     for copy in tok_halo[:2]:
         copy.wait_recv()
-    cot_halo = halo(1)
     enter(1)
     enter(2)
     project(1, 2)

time: 76.5 us -> 75.1 us (0.982)
  Pallas kernels: 75.5 us -> 74.1 us
    pallas_call x1, Pallas kernels: 70.6 us -> 69.2 us  [on_device(): pl.pallas_call(kernel, out_shape=(grid, grid, jax.ShapeDtypeStruct((4, 2,...]
where the time goes in v4:
time: 75.1 us; the launch traced here: 74.9 us
  Pallas kernels  74.1 us (99%)
  between operations  0.8 us (1%)
    pallas_call x1, Pallas kernels, on_device(): pl.pallas_call(kernel, out_shape=(grid, grid, jax.ShapeDtypeStruct((4, 2,...  69.2 us
    pallas_call x1, Pallas kernels, on_device(): pl.pallas_call(unpack_kernel, out_shape=(grid, grid, jax.ShapeDtypeStruct...  4.89 us

profile of v4, /device:TPU:1, one launch (start us, length us, event | category | flops | bytes accessed | tf_op | source)
XLA Modules:
  0.0 74.9 jit_solution(8970867361326566354)
XLA Ops:
  0.6 69.2 %sublayer.1 = (bf16[2,6,48,512]{3,2,1,0:T(8,128)(2,1)}, bf16[2,6,48,512]{3,2,1,0:T(8,128)(2,1)}, bf16[4,2,64,16,128]{4,3,2,1,0:T(8,128)(2,1)}, f32[8,128]{1,0:T(8,128)}) custom-call(bf16[2,6,48,512]{3,2,1,0:T(8,128)(2,1)} %tok_hbm.1, bf16[2,6,48,512]{3,2,1,0:T(8,128)(2,1)} %cot_hbm.1, f32[1,512]{1,0:T(1,128)} %bitcast.2, bf16[512,1536]{1,0:T(8,128)(2,1)} %wqkv_hbm.1, ...), custom_call_target="tpu_custom_call" | custom-call | tf_op jit(solution)/shard_map/sublayer/pallas_call | solution.py:579
  69.9 4.9 %results.1 = (bf16[2,6,48,512]{3,2,1,0:T(8,128)(2,1)}, bf16[2,6,48,512]{3,2,1,0:T(8,128)(2,1)}, f32[512,1536]{1,0:T(8,128)}, f32[512,512]{1,0:T(8,128)}, f32[1,512]{1,0:T(1,128)}) custom-call(bf16[2,6,48,512]{3,2,1,0:T(8,128)(2,1)} %get-tuple-element.14.lay_in, bf16[2,6,48,512]{3,2,1,0:T(8,128)(2,1)} %get-tuple-element.15.gtok_in, ...), custom_call_target="tpu_custom_call" | custom-call | tf_op jit(solution)/shard_map/results/pallas_call | solution.py:595

commit v5 on v4

--- a/solution.py
+++ b/solution.py
@@ -463,20 +463,20 @@
     loads["unpack"].wait()
     take_back(0, lay_copies, lay_ref)
     reduce_third(1)
-    gtok_copies = give_back(1, gtok.astype(BF16))
     spread_third(0)
     gain_send("z", gain_z, gain_take("y", gain_y, 3), 6)
     spread_third(1)
+    gtok_copies = give_back(1, gtok.astype(BF16))
     spread_second(0)
     spread_second(1)
     spread_first(0)
     spread_first(1)
     spread_first(2)
     spread_first(3)
-    take_back(1, gtok_copies, gtok_ref)
     ggain_ref[...] = gain_take("z", gain_z, 6) * factor
     spread_pair(0)
     spread_pair(1)
+    take_back(1, gtok_copies, gtok_ref)
     spread_pair(2)
     spread_pair(3)
     for group in range(4):

time: 75.1 us -> 75.1 us (level)
  no operation moved by 1% of the time
where the time goes in v5:
time: 75.1 us; the launch traced here: 75 us
  Pallas kernels  74.2 us (99%)
  between operations  0.8 us (1%)
    pallas_call x1, Pallas kernels, on_device(): pl.pallas_call(kernel, out_shape=(grid, grid, jax.ShapeDtypeStruct((4, 2,...  69.3 us
    pallas_call x1, Pallas kernels, on_device(): pl.pallas_call(unpack_kernel, out_shape=(grid, grid, jax.ShapeDtypeStruct...  4.89 us

profile of v5, /device:TPU:1, one launch (start us, length us, event | category | flops | bytes accessed | tf_op | source)
XLA Modules:
  0.0 75.0 jit_solution(1370629098780472418)
XLA Ops:
  0.6 69.3 %sublayer.1 = (bf16[2,6,48,512]{3,2,1,0:T(8,128)(2,1)}, bf16[2,6,48,512]{3,2,1,0:T(8,128)(2,1)}, bf16[4,2,64,16,128]{4,3,2,1,0:T(8,128)(2,1)}, f32[8,128]{1,0:T(8,128)}) custom-call(bf16[2,6,48,512]{3,2,1,0:T(8,128)(2,1)} %tok_hbm.1, bf16[2,6,48,512]{3,2,1,0:T(8,128)(2,1)} %cot_hbm.1, f32[1,512]{1,0:T(1,128)} %bitcast.2, bf16[512,1536]{1,0:T(8,128)(2,1)} %wqkv_hbm.1, ...), custom_call_target="tpu_custom_call" | custom-call | tf_op jit(solution)/shard_map/sublayer/pallas_call | solution.py:579
  69.9 4.9 %results.1 = (bf16[2,6,48,512]{3,2,1,0:T(8,128)(2,1)}, bf16[2,6,48,512]{3,2,1,0:T(8,128)(2,1)}, f32[512,1536]{1,0:T(8,128)}, f32[512,512]{1,0:T(8,128)}, f32[1,512]{1,0:T(1,128)}) custom-call(bf16[2,6,48,512]{3,2,1,0:T(8,128)(2,1)} %get-tuple-element.14.lay_in, bf16[2,6,48,512]{3,2,1,0:T(8,128)(2,1)} %get-tuple-element.15.gtok_in, ...), custom_call_target="tpu_custom_call" | custom-call | tf_op jit(solution)/shard_map/results/pallas_call | solution.py:595
